TPU v7x, 32 devices: a whole 2x2x4 slice. The times are simulated.
32 devices in a mesh: dp: 2 (over x), orient: 16 (over z, y, core).
Axes of the slice: x: 2, y: 2, z: 4, core: 2. Of those that a mesh axis runs over, the one named last changes fastest.
Arguments:
- images: bfloat16 [384, 16384], P(('dp', 'orient')), may hold values from -80 to 80
- templates: bfloat16 [4096, 16384], P('orient'), as said below
- index: int32 [4096, 128], P('orient'), may hold values from 0 to 16383
- interp: float32 [4096, 128], P('orient'), may hold values from 0.25 to 1
- inv_noise: float32 [128, 128], replicated, may hold values from 0.5 to 2, as said below
Outputs:
- recon: float32 [16384, 128], P(('dp', 'orient'))
- recon_weight: float32 [16384, 128], P(('dp', 'orient'))
Inputs may be any that keep to these rules, and one draw needn't show every extreme that they name: `templates`: every entry has magnitude at most 18 / 128. `inv_noise`: every entry is 0.5, 1 or 2.
All inputs are finite; a program needn't handle non-finite values.
Results may differ from a plain program's by a relative error of at most 0.0029.
Values may be sent and summed in bfloat16 or wider, within the bound.
A program may use at most 128 MiB of HBM per device.

v0:
```python
import functools

import jax
import jax.numpy as jnp
from jax import lax
from jax.experimental import pallas as pl
from jax.experimental.pallas import tpu as pltpu
from jax.sharding import PartitionSpec as P

LANES = 128
ROWS_STEP = 8
ACCS = 4
UNROLL = 16
LOW_BITS = 5
LOW = 1 << LOW_BITS
VMEM_LIMIT = 56 * 2**20


def data_kernel(post_ref, images_ref, interp_ref, idx_ref, out_ref, rows_ref, *more):
    accs = (out_ref,) + more
    step = pl.program_id(0)
    count, side = post_ref.shape[0], out_ref.shape[1]
    volume_rows = out_ref.shape[0]

    @pl.when(step == 0)
    def _():
        @pl.loop(0, volume_rows // 64)
        def _(c):
            rows = pl.ds(pl.multiple_of(c * 64, 64), 64)
            for acc in accs:
                acc[rows, :] = jnp.zeros((64, side), jnp.float32)

    for j in range(ROWS_STEP):
        block = jnp.dot(
            post_ref[...],
            images_ref[:, j * side : (j + 1) * side],
            preferred_element_type=jnp.float32,
        )
        rows_ref[j * count : (j + 1) * count, :] = block * interp_ref[0, :, j : j + 1]

    @pl.loop(0, ROWS_STEP * count // UNROLL)
    def _(g):
        base = pl.multiple_of(g * UNROLL, UNROLL)
        for k in range(0, UNROLL, ACCS):
            voxels = [idx_ref[0, 0, base + k + a] for a in range(ACCS)]
            summed = [
                accs[a][pl.ds(voxels[a], 1), :] + rows_ref[pl.ds(base + k + a, 1), :]
                for a in range(ACCS)
            ]
            for a in range(ACCS):
                accs[a][pl.ds(voxels[a], 1), :] = summed[a]

    @pl.when(step == pl.num_programs(0) - 1)
    def _():
        @pl.loop(0, volume_rows // 64)
        def _(c):
            rows = pl.ds(pl.multiple_of(c * 64, 64), 64)
            total = accs[0][rows, :]
            for acc in accs[1:]:
                total = total + acc[rows, :]
            out_ref[rows, :] = total


def insert_data(post, gathered, interp_t, index_t, volume_rows):
    count, images = post.shape
    side = interp_t.shape[0]
    steps = side // ROWS_STEP
    interp_b = interp_t.reshape(steps, ROWS_STEP, count).transpose(0, 2, 1)
    index_b = index_t.reshape(steps, 1, ROWS_STEP * count)
    return pl.pallas_call(
        data_kernel,
        grid=(steps,),
        out_shape=jax.ShapeDtypeStruct((volume_rows, side), jnp.float32),
        in_specs=[
            pl.BlockSpec((count, images), lambda i: (0, 0)),
            pl.BlockSpec((images, ROWS_STEP * side), lambda i: (0, i)),
            pl.BlockSpec((1, count, ROWS_STEP), lambda i: (i, 0, 0)),
            pl.BlockSpec(
                (1, 1, ROWS_STEP * count), lambda i: (i, 0, 0), memory_space=pltpu.SMEM
            ),
        ],
        out_specs=pl.BlockSpec(
            (volume_rows, side), lambda i: (0, 0), pipeline_mode=pl.Buffered(1)
        ),
        scratch_shapes=[pltpu.VMEM((ROWS_STEP * count, side), jnp.float32)]
        + [pltpu.VMEM((volume_rows, side), jnp.float32)] * (ACCS - 1),
        compiler_params=pltpu.CompilerParams(vmem_limit_bytes=VMEM_LIMIT),
        cost_estimate=pl.CostEstimate(
            flops=200_000_000_000, bytes_accessed=200_000_000, transcendentals=0
        ),
    )(post, gathered, interp_b, index_b)


def reduce_kernel(
    groups,
    orient,
    blocks_ref,
    mass_ref,
    places_ref,
    noise_ref,
    out_ref,
    weight_ref,
    grid_ref,
    mass_row,
    mine,
    theirs,
    ready,
    landed,
    masses,
    own_sem,
    pair_send,
    pair_recv,
    send_sem,
    recv_sem,
    mass_send,
    mass_recv,
):
    half = orient // 2
    chips = groups * half
    group, place = lax.axis_index("dp"), lax.axis_index("orient")
    core = lax.rem(place, 2)
    me = group * half + lax.div(place, 2)
    partner = (group, place + 1 - 2 * core)
    mesh_ids = pl.DeviceIdType.MESH

    def device(chip):
        return (lax.div(chip, half), lax.rem(chip, half) * 2 + core)

    devices = 2 * chips
    rank = group * orient + place

    def ranked(d):
        return (lax.div(d, orient), lax.rem(d, orient))

    barrier = pltpu.get_barrier_semaphore()

    @pl.loop(1, devices)
    def _(s):
        pl.semaphore_signal(
            barrier,
            inc=1,
            device_id=ranked(lax.rem(rank + s, devices)),
            device_id_type=mesh_ids,
        )

    pl.semaphore_wait(barrier, devices - 1)

    def mass_copy(s):
        return pltpu.make_async_remote_copy(
            src_ref=mass_ref,
            dst_ref=masses.at[s],
            send_sem=mass_send.at[s],
            recv_sem=mass_recv.at[s],
            device_id=ranked(lax.rem(rank + s, devices)),
            device_id_type=mesh_ids,
        )

    def own_copy(s):
        return pltpu.make_async_copy(
            blocks_ref.at[lax.rem(me + s, chips), core], mine.at[s], own_sem.at[s]
        )

    def pair_copy(s):
        return pltpu.make_async_remote_copy(
            src_ref=blocks_ref.at[lax.rem(me + s, chips), 1 - core],
            dst_ref=theirs.at[s],
            send_sem=pair_send.at[s],
            recv_sem=pair_recv.at[s],
            device_id=partner,
            device_id_type=mesh_ids,
        )

    def chip_copy(s):
        return pltpu.make_async_remote_copy(
            src_ref=ready.at[s],
            dst_ref=landed.at[s],
            send_sem=send_sem.at[s],
            recv_sem=recv_sem.at[s],
            device_id=device(lax.rem(me + s, chips)),
            device_id_type=mesh_ids,
        )

    @pl.loop(1, devices)
    def _(s):
        mass_copy(s).start()

    @pl.loop(1, chips + 1)
    def _(k):
        s = lax.rem(k, chips)
        own_copy(s).start()
        pair_copy(s).start()

    @pl.loop(1, chips)
    def _(s):
        own_copy(s).wait()
        pair_copy(s).wait()
        ready[s] = (mine[s] + theirs[s]).astype(ready.dtype)
        chip_copy(s).start()

    own_copy(0).wait()
    pair_copy(0).wait()
    out_ref[...] = mine[0] + theirs[0]
    mass_row[...] = jnp.zeros_like(mass_row)
    mass_rows = mass_ref.shape[0]

    def add_mass(d, ref):
        start = lax.rem(d, orient) * (mass_rows * LANES)
        for k in range(mass_rows):
            lanes = pl.ds(pl.multiple_of(start + k * LANES, LANES), LANES)
            mass_row[:, lanes] += ref[k : k + 1, :]

    add_mass(rank, mass_ref)

    @pl.loop(1, devices)
    def _(s):
        mass_copy(s).wait()
        add_mass(lax.rem(rank + devices - s, devices), masses.at[s])

    insert_weights(rank, places_ref, mass_row, noise_ref, weight_ref, grid_ref)

    @pl.loop(1, chips)
    def _(s):
        chip_copy(s).wait()
        out_ref[...] += landed[s].astype(jnp.float32)


def reduce_rows(volume, mass, places_t, inv_noise, groups, orient):
    chips = groups * orient // 2
    rows, side = volume.shape[0] // (2 * chips), volume.shape[1]
    parts = (chips, rows, side)
    mass_rows = mass.reshape(-1, LANES)
    masses = (2 * chips,) + mass_rows.shape
    return pl.pallas_call(
        functools.partial(reduce_kernel, groups, orient),
        out_shape=(
            jax.ShapeDtypeStruct((rows, side), jnp.float32),
            jax.ShapeDtypeStruct((rows, side), jnp.float32),
        ),
        in_specs=[pl.BlockSpec(memory_space=pl.ANY)]
        + [pl.BlockSpec(memory_space=pltpu.VMEM)] * 3,
        out_specs=(
            pl.BlockSpec(memory_space=pltpu.VMEM),
            pl.BlockSpec(memory_space=pltpu.VMEM),
        ),
        scratch_shapes=[
            pltpu.VMEM((side * max(8, rows // LOW), LANES), jnp.float32),
            pltpu.VMEM((1, places_t.shape[1]), jnp.float32),
        ]
        + [pltpu.VMEM(parts, jnp.float32)] * 2
        + [pltpu.VMEM(parts, jnp.bfloat16)] * 2
        + [pltpu.VMEM(masses, jnp.float32)]
        + [pltpu.SemaphoreType.DMA((chips,))] * 5
        + [pltpu.SemaphoreType.DMA((2 * chips,))] * 2,
        compiler_params=pltpu.CompilerParams(
            collective_id=0, has_side_effects=True, vmem_limit_bytes=VMEM_LIMIT
        ),
    )(volume.reshape(chips, 2, rows, side), mass_rows, places_t, inv_noise)


def split(value):
    high = value.astype(jnp.bfloat16)
    return high, (value - high.astype(jnp.float32)).astype(jnp.bfloat16)


def insert_weights(rank, places_ref, mass_row, noise_ref, out_ref, grid_ref):
    first = rank * out_ref.shape[0]
    count = places_ref.shape[1]
    side = noise_ref.shape[0]
    high_rows = grid_ref.shape[0] // side
    nt = (((1,), (1,)), ((), ()))
    tn = (((0,), (0,)), ((), ()))
    one, zero = jnp.float32(1), jnp.float32(0)

    @pl.loop(0, side // ROWS_STEP)
    def _(step):
        iota_high = lax.broadcasted_iota(jnp.int32, (high_rows, count), 0)
        iota_low = lax.broadcasted_iota(jnp.int32, (LOW, count), 0)
        block = pl.ds(pl.multiple_of(step * ROWS_STEP, ROWS_STEP), ROWS_STEP)
        below = pl.ds(pl.multiple_of(side + step * ROWS_STEP, ROWS_STEP), ROWS_STEP)
        locals_ = places_ref[block, :].astype(jnp.int32) - first
        weights = places_ref[below, :] * mass_row[...]
        for j in range(ROWS_STEP):
            local = locals_[j : j + 1, :]
            hot = jnp.where(iota_high == (local >> LOW_BITS), one, zero)
            low = jnp.where(iota_low == (local & (LOW - 1)), weights[j : j + 1, :], zero)
            part = lax.dot_general(
                hot.astype(jnp.bfloat16),
                low.astype(jnp.bfloat16),
                nt,
                preferred_element_type=jnp.float32,
            )
            row = pl.multiple_of((step * ROWS_STEP + j) * high_rows, 8)
            grid_ref[pl.ds(row, high_rows), :LOW] = part

    noise = noise_ref[...].astype(jnp.bfloat16)
    for h in range(out_ref.shape[0] // LOW):
        high, low = split(grid_ref[pl.ds(h, side, stride=high_rows), :])
        block = lax.dot_general(
            high, noise, tn, preferred_element_type=jnp.float32
        ) + lax.dot_general(low, noise, tn, preferred_element_type=jnp.float32)
        out_ref[h * LOW : (h + 1) * LOW, :] = block[:LOW]


def stats_kernel(orient, own_ref, out_ref, landed, send_sem, recv_sem):
    group, place = lax.axis_index("dp"), lax.axis_index("orient")
    mesh_ids = pl.DeviceIdType.MESH
    barrier = pltpu.get_barrier_semaphore()

    @pl.loop(1, orient)
    def _(s):
        pl.semaphore_signal(
            barrier,
            inc=1,
            device_id=(group, lax.rem(place + s, orient)),
            device_id_type=mesh_ids,
        )

    pl.semaphore_wait(barrier, orient - 1)

    def copy(s):
        return pltpu.make_async_remote_copy(
            src_ref=own_ref,
            dst_ref=landed.at[s],
            send_sem=send_sem.at[s],
            recv_sem=recv_sem.at[s],
            device_id=(group, lax.rem(place + s, orient)),
            device_id_type=mesh_ids,
        )

    @pl.loop(1, orient)
    def _(s):
        copy(s).start()

    out_ref[place] = own_ref[...]

    @pl.loop(1, orient)
    def _(s):
        copy(s).wait()
        out_ref[lax.rem(place + orient - s, orient)] = landed[s]


def gather_stats(own, orient):
    count = own.shape[1]
    pad = -count % (8 * LANES)
    rows = jnp.pad(own, ((0, 0), (0, pad))).reshape(-1, LANES)
    stats = pl.pallas_call(
        functools.partial(stats_kernel, orient),
        out_shape=jax.ShapeDtypeStruct((orient,) + rows.shape, jnp.float32),
        in_specs=[pl.BlockSpec(memory_space=pltpu.VMEM)],
        out_specs=pl.BlockSpec(memory_space=pltpu.VMEM),
        scratch_shapes=[pltpu.VMEM((orient,) + rows.shape, jnp.float32)]
        + [pltpu.SemaphoreType.DMA((orient,))] * 2,
        compiler_params=pltpu.CompilerParams(
            collective_id=1, has_side_effects=True, vmem_limit_bytes=16 * 2**20
        ),
    )(rows)
    return stats.reshape(orient, 2, -1)[:, :, :count]


def shards(groups, orient, images, templates, index, interp, inv_noise):
    side = inv_noise.shape[0]
    volume_rows = side * side
    noise_flat = inv_noise.reshape(-1)
    index_t, interp_t = index.T, interp.T
    gathered = lax.all_gather(images, "orient", axis=0, tiled=True)
    places = jnp.concatenate([index.astype(jnp.float32), interp], axis=1)
    gathered, places = lax.optimization_barrier((gathered, places))
    places_all = lax.all_gather(places, "orient", axis=0, tiled=True)
    tpl_f = templates.astype(jnp.float32)
    weighted = (tpl_f * noise_flat[None, :]).astype(jnp.bfloat16)
    tnorm = 0.5 * jnp.sum(tpl_f * tpl_f * noise_flat[None, :], axis=1)
    scores = (
        lax.dot_general(
            weighted, gathered, (((1,), (1,)), ((), ())), preferred_element_type=jnp.float32
        )
        - tnorm[:, None]
    )
    peak_own = jnp.max(scores, axis=0)
    expo = jnp.exp(scores - peak_own[None, :])
    stats = gather_stats(jnp.stack([peak_own, jnp.sum(expo, axis=0)]), orient)
    peak = jnp.max(stats[:, 0], axis=0)
    total = jnp.sum(stats[:, 1] * jnp.exp(stats[:, 0] - peak[None, :]), axis=0)
    posterior = expo * (jnp.exp(peak_own - peak) / total)[None, :]
    mass = jnp.sum(posterior, axis=1)
    data_vol = insert_data(
        posterior.astype(jnp.bfloat16), gathered, interp_t, index_t, volume_rows
    )
    return reduce_rows(
        data_vol,
        mass,
        places_all.T,
        inv_noise,
        groups,
        orient,
    )


def solution(mesh):
    placed = (
        P(("dp", "orient"), None),
        P("orient", None),
        P("orient", None),
        P("orient", None),
        P(),
    )
    return jax.shard_map(
        functools.partial(shards, mesh.shape["dp"], mesh.shape["orient"]),
        mesh=mesh,
        in_specs=placed,
        out_specs=(P(("dp", "orient"), None), P(("dp", "orient"), None)),
        check_vma=False,
    )
```

profile of v0, /device:TPU:12, one launch (start us, length us, event | category | flops | bytes accessed | tf_op | source)
XLA Modules:
  0.0 240.5 jit_solution(4383444148306686878)
XLA Ops:
  7.2 0.0 all-gather.6.cloned.1.call-start
  7.2 0.7 all-gather.6.cloned.1.call-update
  7.9 0.0 all-gather.4.cloned.1.call-start
  7.9 1.0 copy.20
  8.9 1.0 copy.19
  10.0 1.9 copy.24
  11.9 1.0 copy.25
  12.9 0.8 reshape.40.idx_ref
  13.7 0.7 pad_maximum_fusion
  14.4 5.7 %fusion.2 = f32[256]{0:T(256)S(1)} fusion(bf16[256,16384]{1,0:T(8,128)(2,1)} %param.6, f32[16384]{0:T(1024)} %bitcast.31), kind=kLoop, calls=%fused_computation.4 | loop fusion | flops 16776960 | bytes 8455168 | tf_op jit(solution)/shard_map/reduce_sum | solution.py:371
  20.1 0.0 copy-start
  20.1 64.6 %all-gather.6.cloned.1.call-done = bf16[16,12,16384]{2,1,0:T(8,128)(2,1)} async-done(((bf16[1,12,16384]{2,1,0:T(8,128)(2,1)}), bf16[16,12,16384]{2,1,0:T(8,128)(2,1)}) %all-gather.6.cloned.1.call-update) | async-done | bytes 6291472 | tf_op jit(solution)/shard_map/all_gather | solution.py:365
  84.7 8.8 %reshape.44.images_ref = bf16[192,16384]{1,0:T(8,128)(2,1)} reshape(bf16[16,12,16384]{2,1,0:T(8,128)(2,1)} %all-gather.6.cloned.1.call-done) | data formatting | bytes 12582912 | tf_op jit(solution)/shard_map/optimization_barrier | solution.py:367
  93.5 0.0 copy-done
  93.5 7.5 %fusion.14 = (f32[192]{0:T(256)S(1)}, f32[256,192]{1,0:T(8,128)S(1)}) fusion(f32[256]{0:T(256)S(1)} %broadcast_multiply_fusion, bf16[192,16384]{1,0:T(8,128)(2,1)} %reshape.44.images_ref, bf16[256,16384]{1,0:T(8,128)(2,1)} %param.6, f32[16384]{0:T(1024)S(1)} %bitcast.32), kind=kOutput, calls=%fused_computation.22 | convolution fusion | flops 1623293696 | bytes 14944000 | tf_op jit(solution)/shard_map/dot_general | solution.py:373
  101.0 0.1 fusion.9
  101.1 7.6 %shard_map.68 = f32[16,16,128]{2,1,0:T(8,128)S(1)} custom-call(f32[16,128]{1,0:T(8,128)S(1)} %reshape.37.own_ref), custom_call_target="tpu_custom_call" | custom-call | tf_op jit(solution)/shard_map/pallas_call | solution.py:346
  108.8 0.1 reshape.38
  108.9 1.3 multiply_reduce_fusion
  110.2 0.0 all-gather.4.cloned.1.call-update
  110.2 62.6 %shard_map.69 = f32[16384,128]{1,0:T(8,128)} custom-call(bf16[256,192]{1,0:T(8,128)(2,1)} %get-tuple-element.7.post_ref, bf16[192,16384]{1,0:T(8,128)(2,1)} %reshape.44.images_ref, f32[16,256,8]{2,1,0:T(8,128)} %bitcast.27, s32[16,1,2048]{2,1,0:T(1,128)} %reshape.40.idx_ref), custom_call_target="tpu_custom_call" | custom-call | flops 199999995904 | bytes 200000000 | tf_op jit(solution)/shard_map/pallas_call | solution.py:70
  172.8 0.0 all-gather.4.cloned.1.call-done
  172.8 57.5 %shard_map.70 = (f32[512,128]{1,0:T(8,128)}, f32[512,128]{1,0:T(8,128)}) custom-call(f32[16,2,512,128]{3,2,1,0:T(8,128)} %bitcast.25, f32[2,128]{1,0:T(2,128)} %bitcast.34, f32[256,4096]{1,0:T(8,128)} %bitcast.26, f32[128,128]{1,0:T(8,128)} %noise_ref.1), custom_call_target="tpu_custom_call" | custom-call | tf_op jit(solution)/shard_map/pallas_call | solution.py:233
  230.3 1.7 copy.42
  232.0 1.7 copy.43
  (7 shorter events, 0.1 us)
Async XLA Ops:
  7.2 77.5 %all-gather.6.cloned.1.call-start = ((), (), s32[]{:S(2)}) async-start(), calls=%async_computation.1 | async-start | bytes 8912896 | tf_op jit(solution)/shard_map/all_gather | solution.py:365
  7.9 164.9 %all-gather.4.cloned.1.call-start = ((), (), s32[]{:S(2)}) async-start(), calls=%async_computation | async-start | bytes 4456448 | tf_op jit(solution)/shard_map/all_gather | solution.py:368
  20.1 73.4 %copy-start = (f32[128,128]{1,0:T(8,128)S(1)}, f32[128,128]{1,0:T(8,128)}, u32[]{:S(2)}) copy-start(f32[128,128]{1,0:T(8,128)} %noise_ref.1) | copy-start | bytes 196612
Sparse Core Ops, SparseCore 0:
  10.2 74.4 all-gather.5
  110.4 50.8 all-gather.3
where the time goes:
time: 241 us
  Pallas kernels  128 us (53%)
  waiting for transfers between devices  65.3 us (27%)
  local copies, waits for them, and re-layouts  17.9 us (7%)
  between operations  14.1 us (6%)
  other arithmetic  7.85 us (3%)
  matrix products  7.53 us (3%)
    all_gather x1, waiting for transfers between devices, shards(): gathered = lax.all_gather(images, 'orient', axis=0, tiled=True)  64.6 us
    pallas_call x1, Pallas kernels, insert_data(): pl.pallas_call(data_kernel, grid=(steps,), out_shape=jax.ShapeDtypeStruct...  62.6 us
    pallas_call x1, Pallas kernels, reduce_rows(): pl.pallas_call(functools.partial(reduce_kernel, groups, orient), out_shap...  57.5 us
    optimization_barrier x1, local copies, waits for them, and re-layouts, shards(): gathered, places = lax.optimization_barrier((gathered, places))  8.78 us
    pallas_call x1, Pallas kernels, gather_stats(): pl.pallas_call(functools.partial(stats_kernel, orient), out_shape=jax.Sha...  7.64 us
    dot_general x1, matrix products, shards(): lax.dot_general(weighted, gathered, (((1,), (1,)), ((), ())), preferred_e...  7.53 us
    reduce_sum x1, other arithmetic, shards(): tnorm = 0.5 * jnp.sum(tpl_f * tpl_f * noise_flat[None, :], axis=1)  5.67 us
    unnamed x6, local copies, waits for them, and re-layouts  5.34 us
  transfers between devices with their start and end apart: 2, of which 1 were waited for; matrix products, arithmetic and copies ran while one was open for 5% of the time, Pallas kernels for 26%

commit v1 on v0

--- a/solution.py
+++ b/solution.py
@@ -10,17 +10,24 @@
 LANES = 128
 ROWS_STEP = 8
 ACCS = 4
-UNROLL = 16
+SUB = 4
+BATCH = 128
+LINES = 4
+PARTS = 4
+NORM_COLS = 1024
+LEVELS = 65535
+SHIFT = 65536
 LOW_BITS = 5
 LOW = 1 << LOW_BITS
 VMEM_LIMIT = 56 * 2**20
 
 
-def data_kernel(post_ref, images_ref, interp_ref, idx_ref, out_ref, rows_ref, *more):
+def data_kernel(post_ref, images_ref, interp_ref, idx_ref, clash_ref, out_ref, rows_ref, *more):
     accs = (out_ref,) + more
     step = pl.program_id(0)
     count, side = post_ref.shape[0], out_ref.shape[1]
     volume_rows = out_ref.shape[0]
+    halves = count // BATCH
 
     @pl.when(step == 0)
     def _():
@@ -30,25 +37,53 @@
             for acc in accs:
                 acc[rows, :] = jnp.zeros((64, side), jnp.float32)
 
+    interp = pltpu.roll(interp_ref[...], lax.rem(side - step * ROWS_STEP, side), axis=1)
     for j in range(ROWS_STEP):
         block = jnp.dot(
             post_ref[...],
             images_ref[:, j * side : (j + 1) * side],
             preferred_element_type=jnp.float32,
         )
-        rows_ref[j * count : (j + 1) * count, :] = block * interp_ref[0, :, j : j + 1]
-
-    @pl.loop(0, ROWS_STEP * count // UNROLL)
+        rows_ref[j * count : (j + 1) * count, :] = block * interp[:, j : j + 1]
+
+    @pl.loop(0, ROWS_STEP * halves)
     def _(g):
-        base = pl.multiple_of(g * UNROLL, UNROLL)
-        for k in range(0, UNROLL, ACCS):
-            voxels = [idx_ref[0, 0, base + k + a] for a in range(ACCS)]
-            summed = [
-                accs[a][pl.ds(voxels[a], 1), :] + rows_ref[pl.ds(base + k + a, 1), :]
-                for a in range(ACCS)
-            ]
+        base = pl.multiple_of(g * BATCH, BATCH)
+        voxels = idx_ref.at[g]
+        clash = clash_ref[lax.rem(g, halves), step * ROWS_STEP + lax.div(g, halves)]
+
+        @pl.when(clash == 0)
+        def _():
+            pending = [None] * ACCS
+
+            def flush(a):
+                for voxel, value in pending[a] or ():
+                    accs[a][pl.ds(voxel, 1), :] = value
+
+            for n in range(BATCH // SUB):
+                a = n % ACCS
+                flush(a)
+                pending[a] = []
+                for k in range(n * SUB, (n + 1) * SUB):
+                    voxel = voxels[k]
+                    value = accs[a][pl.ds(voxel, 1), :] + rows_ref[pl.ds(base + k, 1), :]
+                    pending[a].append((voxel, value))
             for a in range(ACCS):
-                accs[a][pl.ds(voxels[a], 1), :] = summed[a]
+                flush(a)
+
+        @pl.when(clash != 0)
+        def _():
+            @pl.loop(0, BATCH // ACCS)
+            def _(q):
+                first = q * ACCS
+                targets = [voxels[first + a] for a in range(ACCS)]
+                summed = [
+                    accs[a][pl.ds(targets[a], 1), :]
+                    + rows_ref[pl.ds(base + first + a, 1), :]
+                    for a in range(ACCS)
+                ]
+                for a in range(ACCS):
+                    accs[a][pl.ds(targets[a], 1), :] = summed[a]
 
     @pl.when(step == pl.num_programs(0) - 1)
     def _():
@@ -61,12 +96,11 @@
             out_ref[rows, :] = total
 
 
-def insert_data(post, gathered, interp_t, index_t, volume_rows):
+def insert_data(post, gathered, interp, voxels, clash, volume_rows):
     count, images = post.shape
-    side = interp_t.shape[0]
+    side = interp.shape[1]
     steps = side // ROWS_STEP
-    interp_b = interp_t.reshape(steps, ROWS_STEP, count).transpose(0, 2, 1)
-    index_b = index_t.reshape(steps, 1, ROWS_STEP * count)
+    batches = ROWS_STEP * count // BATCH
     return pl.pallas_call(
         data_kernel,
         grid=(steps,),
@@ -74,10 +108,9 @@
         in_specs=[
             pl.BlockSpec((count, images), lambda i: (0, 0)),
             pl.BlockSpec((images, ROWS_STEP * side), lambda i: (0, i)),
-            pl.BlockSpec((1, count, ROWS_STEP), lambda i: (i, 0, 0)),
-            pl.BlockSpec(
-                (1, 1, ROWS_STEP * count), lambda i: (i, 0, 0), memory_space=pltpu.SMEM
-            ),
+            pl.BlockSpec((count, side), lambda i: (0, 0)),
+            pl.BlockSpec((batches, BATCH), lambda i: (i, 0), memory_space=pltpu.SMEM),
+            pl.BlockSpec(memory_space=pltpu.SMEM),
         ],
         out_specs=pl.BlockSpec(
             (volume_rows, side), lambda i: (0, 0), pipeline_mode=pl.Buffered(1)
@@ -88,7 +121,7 @@
         cost_estimate=pl.CostEstimate(
             flops=200_000_000_000, bytes_accessed=200_000_000, transcendentals=0
         ),
-    )(post, gathered, interp_b, index_b)
+    )(post, gathered, interp, voxels, clash)
 
 
 def reduce_kernel(
@@ -224,11 +257,10 @@
         out_ref[...] += landed[s].astype(jnp.float32)
 
 
-def reduce_rows(volume, mass, places_t, inv_noise, groups, orient):
+def reduce_rows(volume, mass_rows, places_t, inv_noise, groups, orient):
     chips = groups * orient // 2
     rows, side = volume.shape[0] // (2 * chips), volume.shape[1]
     parts = (chips, rows, side)
-    mass_rows = mass.reshape(-1, LANES)
     masses = (2 * chips,) + mass_rows.shape
     return pl.pallas_call(
         functools.partial(reduce_kernel, groups, orient),
@@ -244,7 +276,7 @@
         ),
         scratch_shapes=[
             pltpu.VMEM((side * max(8, rows // LOW), LANES), jnp.float32),
-            pltpu.VMEM((1, places_t.shape[1]), jnp.float32),
+            pltpu.VMEM((1, places_t.shape[0] * places_t.shape[2]), jnp.float32),
         ]
         + [pltpu.VMEM(parts, jnp.float32)] * 2
         + [pltpu.VMEM(parts, jnp.bfloat16)] * 2
@@ -264,7 +296,8 @@
 
 def insert_weights(rank, places_ref, mass_row, noise_ref, out_ref, grid_ref):
     first = rank * out_ref.shape[0]
-    count = places_ref.shape[1]
+    blocks, _, each = places_ref.shape
+    count = blocks * each
     side = noise_ref.shape[0]
     high_rows = grid_ref.shape[0] // side
     nt = (((1,), (1,)), ((), ()))
@@ -276,9 +309,9 @@
         iota_high = lax.broadcasted_iota(jnp.int32, (high_rows, count), 0)
         iota_low = lax.broadcasted_iota(jnp.int32, (LOW, count), 0)
         block = pl.ds(pl.multiple_of(step * ROWS_STEP, ROWS_STEP), ROWS_STEP)
-        below = pl.ds(pl.multiple_of(side + step * ROWS_STEP, ROWS_STEP), ROWS_STEP)
-        locals_ = places_ref[block, :].astype(jnp.int32) - first
-        weights = places_ref[below, :] * mass_row[...]
+        words = jnp.concatenate([places_ref[d, block, :] for d in range(blocks)], axis=1)
+        locals_ = (words >> 16) - first
+        weights = (words & (SHIFT - 1)).astype(jnp.float32) * (1 / LEVELS) * mass_row[...]
         for j in range(ROWS_STEP):
             local = locals_[j : j + 1, :]
             hot = jnp.where(iota_high == (local >> LOW_BITS), one, zero)
@@ -301,9 +334,49 @@
         out_ref[h * LOW : (h + 1) * LOW, :] = block[:LOW]
 
 
-def stats_kernel(orient, own_ref, out_ref, landed, send_sem, recv_sem):
+def gather_kernel(
+    orient,
+    images_ref,
+    templates_ref,
+    noise_ref,
+    index_ref,
+    interp_ref,
+    gathered_ref,
+    post_ref,
+    mass_ref,
+    words_ref,
+    rows_ref,
+    clash_ref,
+    raw,
+    weighted,
+    whole,
+    scores,
+    norms,
+    stats,
+    landed,
+    load_sem,
+    store_sem,
+    send_sem,
+    recv_sem,
+    stat_send,
+    stat_recv,
+):
+    lines, across = LINES, orient // (2 * LINES)
     group, place = lax.axis_index("dp"), lax.axis_index("orient")
+    core = lax.rem(place, 2)
+    chip = lax.div(place, 2)
+    row, col = lax.div(chip, across), lax.rem(chip, across)
     mesh_ids = pl.DeviceIdType.MESH
+    block_rows, width = images_ref.shape
+    part = width // PARTS
+    count = templates_ref.shape[0]
+    fold = templates_ref.shape[1] // width
+    line_images = 2 * across * block_rows // fold
+    images = line_images * lines
+
+    def at(r, q, c):
+        return (r * across + q) * 2 + c
+
     barrier = pltpu.get_barrier_semaphore()
 
     @pl.loop(1, orient)
@@ -315,83 +388,298 @@
             device_id_type=mesh_ids,
         )
 
+    def load_copy(k):
+        cols = pl.ds(pl.multiple_of(k * width, width), width)
+        return pltpu.make_async_copy(
+            templates_ref.at[:, cols], weighted.at[:, cols], load_sem.at[k]
+        )
+
+    for k in range(fold):
+        load_copy(k).start()
+
     pl.semaphore_wait(barrier, orient - 1)
 
-    def copy(s):
+    def copy(source, r, q, s, way, target):
+        cols = pl.ds(pl.multiple_of(s * part, part), part)
+        slot = at(r, q, core)
+        ref = images_ref if source is None else raw.at[slot]
         return pltpu.make_async_remote_copy(
-            src_ref=own_ref,
+            src_ref=ref.at[:, cols],
+            dst_ref=raw.at[slot, :, cols],
+            send_sem=send_sem.at[lax.div(slot, 2), s, way],
+            recv_sem=recv_sem.at[slot, s],
+            device_id=(group, target),
+            device_id_type=mesh_ids,
+        )
+
+    def arrived(r, q, c, s):
+        cols = pl.ds(pl.multiple_of(s * part, part), part)
+        slot = at(r, q, c)
+        pltpu.make_async_remote_copy(
+            src_ref=raw.at[slot, :, cols],
+            dst_ref=raw.at[slot, :, cols],
+            send_sem=send_sem.at[0, 0, 0],
+            recv_sem=recv_sem.at[slot, s],
+            device_id=(group, place + 1 - 2 * core),
+            device_id_type=mesh_ids,
+        ).wait_recv()
+
+    def each_send(r, q, s, act, source=raw):
+        for way, step in ((0, 1), (1, -1)):
+            onward = row + step
+            if source is None:
+                along = (onward >= 0) & (onward < lines)
+            else:
+                along = (q == col) & (onward >= 0) & (onward < lines) & ((row - r) * step > 0)
+
+            @pl.when(along)
+            def _(way=way, onward=onward):
+                act(copy(source, r, q, s, way, at(onward, col, core)))
+
+        for way, step in ((2, 1), (3, -1)):
+            onward = col + step
+            beside = (onward >= 0) & (onward < across) & ((col - q) * step >= 0)
+
+            @pl.when(beside)
+            def _(way=way, onward=onward):
+                act(copy(source, r, q, s, way, at(row, onward, core)))
+
+        act(copy(source, r, q, s, 4, place + 1 - 2 * core))
+
+    @pl.loop(0, PARTS)
+    def _(s):
+        each_send(row, col, s, lambda c: c.start(), None)
+
+    raw[place] = images_ref[...]
+    scores[...] = jnp.zeros_like(scores)
+    norms[...] = jnp.zeros_like(norms)
+
+    index = index_ref[...]
+    near = jnp.zeros(index.shape, jnp.int32)
+    spot = lax.broadcasted_iota(jnp.int32, index.shape, 0) % SUB
+    for d in range(1, SUB):
+        same = (index == pltpu.roll(index, d, axis=0)) & (spot >= d)
+        near = near | same.astype(jnp.int32)
+    clash_ref[...] = jnp.zeros_like(clash_ref)
+    for h in range(count // BATCH):
+        clash_ref[h : h + 1, :] = jnp.max(
+            near[h * BATCH : (h + 1) * BATCH, :], axis=0, keepdims=True
+        )
+    index_t = index.T
+    for h in range(count // BATCH):
+        rows_ref[pl.ds(h, index_t.shape[0], stride=count // BATCH), :] = index_t[
+            :, h * BATCH : (h + 1) * BATCH
+        ]
+    level = (interp_ref[...] * LEVELS + 0.5).astype(jnp.int32)
+    words_ref[...] = (index * SHIFT + level).T
+
+    def weigh(k):
+        load_copy(k).wait()
+
+        @pl.loop(0, width // NORM_COLS)
+        def _(g):
+            cols = pl.ds(pl.multiple_of(k * width + g * NORM_COLS, NORM_COLS), NORM_COLS)
+            for h in range(0, count, 64):
+                tpl = weighted[h : h + 64, cols].astype(jnp.float32)
+                noise = noise_ref[:, cols]
+                scaled = tpl * noise
+                square = tpl * tpl * noise
+                total = square[:, :LANES]
+                for j in range(1, NORM_COLS // LANES):
+                    total = total + square[:, j * LANES : (j + 1) * LANES]
+                norms[h : h + 64, :] += total
+                weighted[h : h + 64, cols] = scaled.astype(jnp.bfloat16)
+
+    def score(r, s):
+        for q in range(across):
+            arrived(r, q, 1 - core, s)
+        cols = pl.ds(pl.multiple_of(s * part, part), part)
+        slots = pl.ds(pl.multiple_of(r * (2 * across), 2 * across), 2 * across)
+        block = raw[slots, :, cols].reshape(2 * across * block_rows, part)
+        total = 2 * across * block_rows
+        out_row = lax.broadcasted_iota(jnp.int32, (total, total), 0)
+        from_row = lax.broadcasted_iota(jnp.int32, (total, total), 1)
+        wanted = (out_row % line_images) * fold + out_row // line_images
+        pick = jnp.where(from_row == wanted, 1.0, 0.0).astype(jnp.bfloat16)
+        sorted_ = jnp.dot(pick, block, preferred_element_type=jnp.float32)
+        sorted_ = sorted_.astype(jnp.bfloat16)
+        rows = pl.ds(pl.multiple_of(r * line_images, line_images), line_images)
+        added = scores[rows, :]
+        for k in range(fold):
+            piece = sorted_[k * line_images : (k + 1) * line_images, :]
+            span = pl.ds(pl.multiple_of(k * width + s * part, part), part)
+            whole[rows, span] = piece
+            added = added + lax.dot_general(
+                piece,
+                weighted[:, span],
+                (((1,), (1,)), ((), ())),
+                preferred_element_type=jnp.float32,
+            )
+        scores[rows, :] = added
+
+    def store_copy(r):
+        rows = pl.ds(pl.multiple_of(r * line_images, line_images), line_images)
+        return pltpu.make_async_copy(whole.at[rows], gathered_ref.at[rows], store_sem.at[r])
+
+    def score_store(r, s):
+        score(r, s)
+
+        @pl.when(s == PARTS - 1)
+        def _():
+            store_copy(r).start()
+
+    @pl.loop(0, lines * PARTS + 1)
+    def _(k):
+        n, s = lax.div(k, PARTS) + 1, lax.rem(k, PARTS)
+        for sign in (1, -1):
+            r = row + sign * n
+
+            @pl.when((r >= 0) & (r < lines) & (n < lines))
+            def _(r=r):
+                arrived(r, col, core, s)
+                each_send(r, col, s, lambda c: c.start())
+
+        for sign in (1, -1):
+            r = row + sign * (n - 1)
+            live = (r >= 0) & (r < lines) & (n <= lines)
+            if sign < 0:
+                live = live & (n > 1)
+            for e in range(1, across):
+                for side in (1, -1):
+                    q = col + side * e
+
+                    @pl.when(live & (q >= 0) & (q < across))
+                    def _(r=r, q=q):
+                        arrived(r, q, core, s)
+                        each_send(r, q, s, lambda c: c.start())
+
+        @pl.when(n == 1)
+        def _():
+            @pl.loop(0, fold // PARTS)
+            def _(j):
+                weigh(s * (fold // PARTS) + j)
+
+        last = jnp.maximum(k - 1, 0)
+        m, t = lax.div(last, PARTS) + 1, lax.rem(last, PARTS)
+
+        @pl.when((m == 2) & (k > 0))
+        def _():
+            score_store(row, t)
+
+        for sign in (1, -1):
+            r = row + sign * (m - 1)
+
+            @pl.when((m > 1) & (r >= 0) & (r < lines))
+            def _(r=r):
+                score_store(r, t)
+
+    norm = 0.5 * jnp.sum(norms[...].T, axis=0, keepdims=True)
+    value = (scores[...] - norm).T
+    peak_own = jnp.max(value, axis=0, keepdims=True)
+    expo = jnp.exp(value - peak_own)
+    stats[...] = jnp.zeros_like(stats)
+    stats[0:1, :] = peak_own
+    stats[1:2, :] = jnp.sum(expo, axis=0, keepdims=True)
+
+    def stat_copy(s):
+        return pltpu.make_async_remote_copy(
+            src_ref=stats,
             dst_ref=landed.at[s],
-            send_sem=send_sem.at[s],
-            recv_sem=recv_sem.at[s],
+            send_sem=stat_send.at[s],
+            recv_sem=stat_recv.at[s],
             device_id=(group, lax.rem(place + s, orient)),
             device_id_type=mesh_ids,
         )
 
     @pl.loop(1, orient)
     def _(s):
-        copy(s).start()
-
-    out_ref[place] = own_ref[...]
+        stat_copy(s).start()
+
+    landed[0] = stats[...]
 
     @pl.loop(1, orient)
     def _(s):
-        copy(s).wait()
-        out_ref[lax.rem(place + orient - s, orient)] = landed[s]
-
-
-def gather_stats(own, orient):
-    count = own.shape[1]
-    pad = -count % (8 * LANES)
-    rows = jnp.pad(own, ((0, 0), (0, pad))).reshape(-1, LANES)
-    stats = pl.pallas_call(
-        functools.partial(stats_kernel, orient),
-        out_shape=jax.ShapeDtypeStruct((orient,) + rows.shape, jnp.float32),
-        in_specs=[pl.BlockSpec(memory_space=pltpu.VMEM)],
-        out_specs=pl.BlockSpec(memory_space=pltpu.VMEM),
-        scratch_shapes=[pltpu.VMEM((orient,) + rows.shape, jnp.float32)]
-        + [pltpu.SemaphoreType.DMA((orient,))] * 2,
+        stat_copy(s).wait()
+
+    peak = peak_own
+    for s in range(1, orient):
+        peak = jnp.maximum(peak, landed[s, 0:1, :])
+    total = jnp.zeros_like(peak)
+    for s in range(orient):
+        total = total + landed[s, 1:2, :] * jnp.exp(landed[s, 0:1, :] - peak)
+    posterior = (expo * (jnp.exp(peak_own - peak) / total))[:, :images]
+    post_ref[...] = posterior.astype(jnp.bfloat16)
+    mass = jnp.sum(posterior, axis=1, keepdims=True)
+    mass_ref[...] = jnp.broadcast_to(mass, (count, LANES)).T[:8, :]
+
+    for r in range(lines):
+        store_copy(r).wait()
+
+    @pl.loop(0, PARTS)
+    def _(s):
+        each_send(row, col, s, lambda c: c.wait_send(), None)
+        for r in range(lines):
+            for q in range(across):
+
+                @pl.when((row != r) | (col != q))
+                def _(r=r, q=q):
+                    each_send(r, q, s, lambda c: c.wait_send())
+
+
+def gather_scores(images, templates, index, interp, noise_flat, orient):
+    own, pixels = images.shape
+    count, side = index.shape
+    fold = PARTS
+    while own * fold % 16:
+        fold += PARTS
+    width = pixels // fold
+    total = own * orient
+    padded = -(-total // LANES) * LANES
+    vmem = pl.BlockSpec(memory_space=pltpu.VMEM)
+    hbm = pl.BlockSpec(memory_space=pl.ANY)
+    chips = orient // 2
+    return pl.pallas_call(
+        functools.partial(gather_kernel, orient),
+        out_shape=(
+            jax.ShapeDtypeStruct((total, pixels), jnp.bfloat16),
+            jax.ShapeDtypeStruct((count, total), jnp.bfloat16),
+            jax.ShapeDtypeStruct((8, count), jnp.float32),
+            jax.ShapeDtypeStruct((side, count), jnp.int32),
+            jax.ShapeDtypeStruct((side * count // BATCH, BATCH), jnp.int32),
+            jax.ShapeDtypeStruct((8, side), jnp.int32),
+        ),
+        in_specs=[vmem, hbm, vmem, vmem, vmem],
+        out_specs=(hbm, vmem, vmem, vmem, vmem, vmem),
+        scratch_shapes=[
+            pltpu.VMEM((orient, own * fold, width), jnp.bfloat16),
+            pltpu.VMEM((count, pixels), jnp.bfloat16),
+            pltpu.VMEM((total, pixels), jnp.bfloat16),
+            pltpu.VMEM((padded, count), jnp.float32),
+            pltpu.VMEM((count, LANES), jnp.float32),
+            pltpu.VMEM((8, padded), jnp.float32),
+            pltpu.VMEM((orient, 8, padded), jnp.float32),
+            pltpu.SemaphoreType.DMA((fold,)),
+            pltpu.SemaphoreType.DMA((LINES,)),
+            pltpu.SemaphoreType.DMA((chips, PARTS, 5)),
+            pltpu.SemaphoreType.DMA((orient, PARTS)),
+            pltpu.SemaphoreType.DMA((orient,)),
+            pltpu.SemaphoreType.DMA((orient,)),
+        ],
         compiler_params=pltpu.CompilerParams(
-            collective_id=1, has_side_effects=True, vmem_limit_bytes=16 * 2**20
+            collective_id=1, has_side_effects=True, vmem_limit_bytes=VMEM_LIMIT
         ),
-    )(rows)
-    return stats.reshape(orient, 2, -1)[:, :, :count]
+    )(images.reshape(own * fold, width), templates, noise_flat, index, interp)
 
 
 def shards(groups, orient, images, templates, index, interp, inv_noise):
     side = inv_noise.shape[0]
-    volume_rows = side * side
-    noise_flat = inv_noise.reshape(-1)
-    index_t, interp_t = index.T, interp.T
-    gathered = lax.all_gather(images, "orient", axis=0, tiled=True)
-    places = jnp.concatenate([index.astype(jnp.float32), interp], axis=1)
-    gathered, places = lax.optimization_barrier((gathered, places))
-    places_all = lax.all_gather(places, "orient", axis=0, tiled=True)
-    tpl_f = templates.astype(jnp.float32)
-    weighted = (tpl_f * noise_flat[None, :]).astype(jnp.bfloat16)
-    tnorm = 0.5 * jnp.sum(tpl_f * tpl_f * noise_flat[None, :], axis=1)
-    scores = (
-        lax.dot_general(
-            weighted, gathered, (((1,), (1,)), ((), ())), preferred_element_type=jnp.float32
-        )
-        - tnorm[:, None]
+    gathered, post, mass, words, voxels, clash = gather_scores(
+        images, templates, index, interp, inv_noise.reshape(1, -1), orient
     )
-    peak_own = jnp.max(scores, axis=0)
-    expo = jnp.exp(scores - peak_own[None, :])
-    stats = gather_stats(jnp.stack([peak_own, jnp.sum(expo, axis=0)]), orient)
-    peak = jnp.max(stats[:, 0], axis=0)
-    total = jnp.sum(stats[:, 1] * jnp.exp(stats[:, 0] - peak[None, :]), axis=0)
-    posterior = expo * (jnp.exp(peak_own - peak) / total)[None, :]
-    mass = jnp.sum(posterior, axis=1)
-    data_vol = insert_data(
-        posterior.astype(jnp.bfloat16), gathered, interp_t, index_t, volume_rows
-    )
+    places = lax.all_gather(words, "orient", axis=0)
+    volume = insert_data(post, gathered, interp, voxels, clash, side * side)
     return reduce_rows(
-        data_vol,
-        mass,
-        places_all.T,
-        inv_noise,
-        groups,
-        orient,
+        volume, mass[0].reshape(-1, LANES), places, inv_noise, groups, orient
     )
 
 

time: 241 us -> 179 us (0.74)
  the two profiles are of different devices: /device:TPU:12 before, /device:TPU:13 now
where the time goes in v1:
time: 179 us
  Pallas kernels  158 us (88%)
  between operations  14 us (8%)
  local copies, waits for them, and re-layouts  6.7 us (4%)
    pallas_call x1, Pallas kernels, reduce_rows(): pl.pallas_call(functools.partial(reduce_kernel, groups, orient), out_shap...  57.2 us
    pallas_call x1, Pallas kernels, gather_scores(): pl.pallas_call(functools.partial(gather_kernel, orient), out_shape=(jax.S...  50.6 us
    pallas_call x1, Pallas kernels, insert_data(): pl.pallas_call(data_kernel, grid=(steps,), out_shape=jax.ShapeDtypeStruct...  50.4 us
  transfers between devices with their start and end apart: 1, of which 0 were waited for; matrix products, arithmetic and copies ran while one was open for 1% of the time, Pallas kernels for 28%

profile of v1, /device:TPU:13, one launch (start us, length us, event | category | flops | bytes accessed | tf_op | source)
XLA Modules:
  0.0 179.1 jit_solution(10118385130108282188)
XLA Ops:
  7.2 0.0 all-gather.3.cloned.1.call-start
  7.2 2.1 %reshape.13.images_ref = bf16[48,4096]{1,0:T(8,128)(2,1)} reshape(bf16[12,16384]{1,0:T(8,128)(2,1)} %param.5) | data formatting | bytes 786432 | tf_op jit(solution)/shard_map/reshape | solution.py:671
  9.3 50.6 %shard_map.68 = (bf16[192,16384]{1,0:T(8,128)(2,1)}, bf16[256,192]{1,0:T(8,128)(2,1)}, f32[8,256]{1,0:T(8,128)}, s32[128,256]{1,0:T(8,128)}, s32[256,128]{1,0:T(8,128)}, /*index=5*/s32[8,128]{1,0:T(8,128)}) custom-call(bf16[48,4096]{1,0:T(8,128)(2,1)} %reshape.13.images_ref, bf16[256,16384]{1,0:T(8,128)(2,1)} %templates_ref.1, f32[1,16384]{1,0:T(1,128)} %bitcast.6, ...), custom_call_target="tpu_custom_call" | custom-call | tf_op jit(solution)/shard_map/pallas_call | solution.py:641
  59.9 0.0 all-gather.3.cloned.1.call-update
  59.9 50.4 %shard_map.69 = f32[16384,128]{1,0:T(8,128)} custom-call(bf16[256,192]{1,0:T(8,128)(2,1)} %get-tuple-element.8.post_ref, bf16[192,16384]{1,0:T(8,128)(2,1)} %get-tuple-element.9.images_ref, f32[256,128]{1,0:T(8,128)} %interp_ref.3, s32[256,128]{1,0:T(8,128)} %get-tuple-element.10.idx_ref, s32[8,128]{1,0:T(8,128)} %get-tuple-element.11.clash_ref), custom_call_target="tpu_custom_call" | custom-call | flops 199999995904 | bytes 200000000 | tf_op jit(solution)/shard_map/pallas_call | solution.py:104
  110.4 1.3 slice.3
  111.6 0.0 all-gather.3.cloned.1.call-done
  111.6 57.2 %shard_map.70 = (f32[512,128]{1,0:T(8,128)}, f32[512,128]{1,0:T(8,128)}) custom-call(f32[16,2,512,128]{3,2,1,0:T(8,128)} %bitcast.4, f32[2,128]{1,0:T(2,128)} %bitcast.7, s32[16,128,256]{2,1,0:T(8,128)} %bitcast.5, f32[128,128]{1,0:T(8,128)} %noise_ref.1), custom_call_target="tpu_custom_call" | custom-call | tf_op jit(solution)/shard_map/pallas_call | solution.py:265
  168.9 1.7 copy.9
  170.5 1.7 copy.10
Async XLA Ops:
  7.2 104.5 %all-gather.3.cloned.1.call-start = ((), (), s32[]{:S(2)}) async-start(), calls=%async_computation | async-start | bytes 2228224 | tf_op jit(solution)/shard_map/all_gather | solution.py:679
Sparse Core Ops, SparseCore 0:
  60.0 41.0 all-gather.2

commit v2 on v1

--- a/solution.py
+++ b/solution.py
@@ -137,33 +137,66 @@
     mass_row,
     mine,
     theirs,
-    ready,
-    landed,
+    first_x,
+    first_x_in,
+    first_y,
+    first_y_in,
+    second_x,
+    second_x_in,
+    second_y,
+    second_y_in,
+    last,
+    last_in,
     masses,
     own_sem,
     pair_send,
     pair_recv,
-    send_sem,
-    recv_sem,
+    fx_send,
+    fx_recv,
+    fy_send,
+    fy_recv,
+    sx_send,
+    sx_recv,
+    sy_send,
+    sy_recv,
+    last_send,
+    last_recv,
     mass_send,
     mass_recv,
 ):
-    half = orient // 2
-    chips = groups * half
+    lines, across = LINES, orient // (2 * LINES)
+    devices = groups * orient
     group, place = lax.axis_index("dp"), lax.axis_index("orient")
-    core = lax.rem(place, 2)
-    me = group * half + lax.div(place, 2)
-    partner = (group, place + 1 - 2 * core)
+    core, chip = lax.rem(place, 2), lax.div(place, 2)
+    row, col = lax.div(chip, across), lax.rem(chip, across)
+    rank = group * orient + place
+    half = out_ref.shape[0] // 2
     mesh_ids = pl.DeviceIdType.MESH
-
-    def device(chip):
-        return (lax.div(chip, half), lax.rem(chip, half) * 2 + core)
-
-    devices = 2 * chips
-    rank = group * orient + place
 
     def ranked(d):
         return (lax.div(d, orient), lax.rem(d, orient))
+
+    def line(k):
+        return lax.rem(row + k + 1, lines)
+
+    def group_at(i):
+        return lax.rem(group + i, groups)
+
+    def col_at(j):
+        return lax.rem(col + j, across)
+
+    def block(x, r, q):
+        return (x * lines + r) * across + q
+
+    def remote(source, target, send, recv, x, r, q, c):
+        return pltpu.make_async_remote_copy(
+            src_ref=source,
+            dst_ref=target,
+            send_sem=send,
+            recv_sem=recv,
+            device_id=(x, (r * across + q) * 2 + c),
+            device_id_type=mesh_ids,
+        )
 
     barrier = pltpu.get_barrier_semaphore()
 
@@ -175,6 +208,19 @@
             device_id=ranked(lax.rem(rank + s, devices)),
             device_id_type=mesh_ids,
         )
+
+    def own_copy(k, i, j):
+        p = block(group_at(i), line(k), col_at(j))
+        return pltpu.make_async_copy(
+            blocks_ref.at[p, core], mine.at[p], own_sem.at[k, i * across + j]
+        )
+
+    for i in reversed(range(groups)):
+        for j in reversed(range(across)):
+
+            @pl.loop(0, lines)
+            def _(k, i=i, j=j):
+                own_copy(k, i, j).start()
 
     pl.semaphore_wait(barrier, devices - 1)
 
@@ -188,51 +234,166 @@
             device_id_type=mesh_ids,
         )
 
-    def own_copy(s):
-        return pltpu.make_async_copy(
-            blocks_ref.at[lax.rem(me + s, chips), core], mine.at[s], own_sem.at[s]
-        )
-
-    def pair_copy(s):
-        return pltpu.make_async_remote_copy(
-            src_ref=blocks_ref.at[lax.rem(me + s, chips), 1 - core],
-            dst_ref=theirs.at[s],
-            send_sem=pair_send.at[s],
-            recv_sem=pair_recv.at[s],
-            device_id=partner,
-            device_id_type=mesh_ids,
-        )
-
-    def chip_copy(s):
-        return pltpu.make_async_remote_copy(
-            src_ref=ready.at[s],
-            dst_ref=landed.at[s],
-            send_sem=send_sem.at[s],
-            recv_sem=recv_sem.at[s],
-            device_id=device(lax.rem(me + s, chips)),
-            device_id_type=mesh_ids,
-        )
+    def pair_copy(k, i, j):
+        p, n = block(group_at(i), line(k), col_at(j)), i * across + j
+        return remote(
+            blocks_ref.at[p, 1 - core],
+            theirs.at[p],
+            pair_send.at[k, n],
+            pair_recv.at[k, n],
+            group,
+            row,
+            col,
+            1 - core,
+        )
+
+    def first_x_copy(k, i):
+        return remote(
+            first_x.at[i - 1, k],
+            first_x_in.at[i - 1, k],
+            fx_send.at[i - 1, k],
+            fx_recv.at[i - 1, k],
+            group_at(i),
+            row,
+            col,
+            core,
+        )
+
+    def first_y_copy(k, j):
+        return remote(
+            first_y.at[j - 1, k],
+            first_y_in.at[j - 1, k],
+            fy_send.at[j - 1, k],
+            fy_recv.at[j - 1, k],
+            group,
+            row,
+            col_at(j),
+            core,
+        )
+
+    def second_x_copy(k, i):
+        return remote(
+            second_x.at[i - 1, k],
+            second_x_in.at[i - 1, k],
+            sx_send.at[i - 1, k],
+            sx_recv.at[i - 1, k],
+            group_at(i),
+            row,
+            col,
+            core,
+        )
+
+    def second_y_copy(k, j):
+        return remote(
+            second_y.at[j - 1, k],
+            second_y_in.at[j - 1, k],
+            sy_send.at[j - 1, k],
+            sy_recv.at[j - 1, k],
+            group,
+            row,
+            col_at(j),
+            core,
+        )
+
+    def last_copy(k):
+        return remote(
+            last.at[k],
+            last_in.at[k],
+            last_send.at[k],
+            last_recv.at[k],
+            group,
+            line(k),
+            col,
+            core,
+        )
+
+    @pl.loop(0, lines)
+    def _(k):
+        for i in reversed(range(groups)):
+            for j in reversed(range(across)):
+                pair_copy(k, i, j).start()
 
     @pl.loop(1, devices)
     def _(s):
         mass_copy(s).start()
 
-    @pl.loop(1, chips + 1)
-    def _(k):
-        s = lax.rem(k, chips)
-        own_copy(s).start()
-        pair_copy(s).start()
-
-    @pl.loop(1, chips)
-    def _(s):
-        own_copy(s).wait()
-        pair_copy(s).wait()
-        ready[s] = (mine[s] + theirs[s]).astype(ready.dtype)
-        chip_copy(s).start()
-
-    own_copy(0).wait()
-    pair_copy(0).wait()
-    out_ref[...] = mine[0] + theirs[0]
+    def narrow(value):
+        return value.astype(jnp.bfloat16)
+
+    def begin(k):
+        for i in reversed(range(groups)):
+            for j in reversed(range(across)):
+                x, q = group_at(i), col_at(j)
+                p = block(x, line(k), q)
+                own_copy(k, i, j).wait()
+                pair_copy(k, i, j).wait()
+                if i == 0 or j == 0:
+                    total = mine[p] + theirs[p]
+                    mine[p] = total
+                    if i:
+                        first_x[i - 1, k, q] = narrow(total[:half])
+                    if j:
+                        first_y[j - 1, k, x] = narrow(total[half:])
+                else:
+                    first_x[i - 1, k, q] = narrow(mine[p, :half] + theirs[p, :half])
+                    first_y[j - 1, k, x] = narrow(mine[p, half:] + theirs[p, half:])
+            if i:
+                first_x_copy(k, i).start()
+        for j in range(1, across):
+            first_y_copy(k, j).start()
+
+    def middle(k):
+        for i in range(1, groups):
+            first_x_copy(k, i).wait()
+        for j in reversed(range(across)):
+            q = col_at(j)
+            p = block(group, line(k), q)
+            total = mine[p, :half]
+            for i in range(1, groups):
+                total = total + first_x_in[i - 1, k, q].astype(jnp.float32)
+            if j:
+                second_y[j - 1, k] = narrow(total)
+                second_y_copy(k, j).start()
+            else:
+                mine[p, :half] = total
+        for j in range(1, across):
+            first_y_copy(k, j).wait()
+        for i in reversed(range(groups)):
+            x = group_at(i)
+            p = block(x, line(k), col)
+            total = mine[p, half:]
+            for j in range(1, across):
+                total = total + first_y_in[j - 1, k, x].astype(jnp.float32)
+            if i:
+                second_x[i - 1, k] = narrow(total)
+                second_x_copy(k, i).start()
+            else:
+                mine[p, half:] = total
+
+    def end(k):
+        p = block(group, line(k), col)
+        for j in range(1, across):
+            second_y_copy(k, j).wait()
+        top = mine[p, :half]
+        for j in range(1, across):
+            top = top + second_y_in[j - 1, k].astype(jnp.float32)
+        for i in range(1, groups):
+            second_x_copy(k, i).wait()
+        low = mine[p, half:]
+        for i in range(1, groups):
+            low = low + second_x_in[i - 1, k].astype(jnp.float32)
+
+        @pl.when(k < lines - 1)
+        def _():
+            last[k, :half] = narrow(top)
+            last[k, half:] = narrow(low)
+            last_copy(k).start()
+
+        @pl.when(k == lines - 1)
+        def _():
+            out_ref[:half] = top
+            out_ref[half:] = low
+
     mass_row[...] = jnp.zeros_like(mass_row)
     mass_rows = mass_ref.shape[0]
 
@@ -242,26 +403,72 @@
             lanes = pl.ds(pl.multiple_of(start + k * LANES, LANES), LANES)
             mass_row[:, lanes] += ref[k : k + 1, :]
 
-    add_mass(rank, mass_ref)
-
-    @pl.loop(1, devices)
-    def _(s):
-        mass_copy(s).wait()
-        add_mass(lax.rem(rank + devices - s, devices), masses.at[s])
-
-    insert_weights(rank, places_ref, mass_row, noise_ref, weight_ref, grid_ref)
-
-    @pl.loop(1, chips)
-    def _(s):
-        chip_copy(s).wait()
-        out_ref[...] += landed[s].astype(jnp.float32)
+    steps, slots = noise_ref.shape[0] // ROWS_STEP, 3 * (lines + 2)
+
+    def weigh(w):
+        weight_step(w, rank * out_ref.shape[0], places_ref, mass_row, grid_ref)
+
+    @pl.loop(0, slots)
+    def _(slot):
+        k, turn = lax.div(slot, 3), lax.rem(slot, 3)
+
+        @pl.when((turn == 0) & (k < lines))
+        def _():
+            begin(k)
+
+        @pl.when((turn == 1) & (k >= 1) & (k < lines + 1))
+        def _():
+            middle(k - 1)
+
+        @pl.when((turn == 2) & (k >= 2))
+        def _():
+            end(k - 2)
+
+        @pl.when(slot == 1)
+        def _():
+            add_mass(rank, mass_ref)
+
+            @pl.loop(1, devices)
+            def _(s):
+                mass_copy(s).wait()
+                add_mass(lax.rem(rank + devices - s, devices), masses.at[s])
+
+        @pl.when((slot >= 2) & (slot < 2 + steps))
+        def _():
+            weigh(slot - 2)
+
+    @pl.loop(slots - 2, max(steps, slots - 2))
+    def _(w):
+        weigh(w)
+
+    weight_rows(noise_ref, weight_ref, grid_ref)
+    for k in range(lines - 1):
+        last_copy(k).wait()
+        out_ref[...] += last_in[k].astype(jnp.float32)
 
 
 def reduce_rows(volume, mass_rows, places_t, inv_noise, groups, orient):
     chips = groups * orient // 2
+    lines, across = LINES, orient // (2 * LINES)
     rows, side = volume.shape[0] // (2 * chips), volume.shape[1]
+    half = rows // 2
     parts = (chips, rows, side)
     masses = (2 * chips,) + mass_rows.shape
+    shapes = [
+        (groups - 1, lines, across, half, side),
+        (across - 1, lines, groups, half, side),
+        (groups - 1, lines, half, side),
+        (across - 1, lines, half, side),
+        (lines - 1, rows, side),
+    ]
+    sems = [
+        (groups - 1, lines),
+        (across - 1, lines),
+        (groups - 1, lines),
+        (across - 1, lines),
+        (lines - 1,),
+        (2 * chips,),
+    ]
     return pl.pallas_call(
         functools.partial(reduce_kernel, groups, orient),
         out_shape=(
@@ -279,10 +486,10 @@
             pltpu.VMEM((1, places_t.shape[0] * places_t.shape[2]), jnp.float32),
         ]
         + [pltpu.VMEM(parts, jnp.float32)] * 2
-        + [pltpu.VMEM(parts, jnp.bfloat16)] * 2
+        + [pltpu.VMEM(s, jnp.bfloat16) for s in shapes for _ in range(2)]
         + [pltpu.VMEM(masses, jnp.float32)]
-        + [pltpu.SemaphoreType.DMA((chips,))] * 5
-        + [pltpu.SemaphoreType.DMA((2 * chips,))] * 2,
+        + [pltpu.SemaphoreType.DMA((lines, groups * across))] * 3
+        + [pltpu.SemaphoreType.DMA(s) for s in sems for _ in range(2)],
         compiler_params=pltpu.CompilerParams(
             collective_id=0, has_side_effects=True, vmem_limit_bytes=VMEM_LIMIT
         ),
@@ -294,37 +501,36 @@
     return high, (value - high.astype(jnp.float32)).astype(jnp.bfloat16)
 
 
-def insert_weights(rank, places_ref, mass_row, noise_ref, out_ref, grid_ref):
-    first = rank * out_ref.shape[0]
-    blocks, _, each = places_ref.shape
+def weight_step(step, first, places_ref, mass_row, grid_ref):
+    blocks, side, each = places_ref.shape
     count = blocks * each
+    high_rows = grid_ref.shape[0] // side
+    nt = (((1,), (1,)), ((), ()))
+    one, zero = jnp.float32(1), jnp.float32(0)
+    iota_high = lax.broadcasted_iota(jnp.int32, (high_rows, count), 0)
+    iota_low = lax.broadcasted_iota(jnp.int32, (LOW, count), 0)
+    block = pl.ds(pl.multiple_of(step * ROWS_STEP, ROWS_STEP), ROWS_STEP)
+    words = jnp.concatenate([places_ref[d, block, :] for d in range(blocks)], axis=1)
+    locals_ = (words >> 16) - first
+    weights = (words & (SHIFT - 1)).astype(jnp.float32) * (1 / LEVELS) * mass_row[...]
+    for j in range(ROWS_STEP):
+        local = locals_[j : j + 1, :]
+        hot = jnp.where(iota_high == (local >> LOW_BITS), one, zero)
+        low = jnp.where(iota_low == (local & (LOW - 1)), weights[j : j + 1, :], zero)
+        part = lax.dot_general(
+            hot.astype(jnp.bfloat16),
+            low.astype(jnp.bfloat16),
+            nt,
+            preferred_element_type=jnp.float32,
+        )
+        row = pl.multiple_of((step * ROWS_STEP + j) * high_rows, 8)
+        grid_ref[pl.ds(row, high_rows), :LOW] = part
+
+
+def weight_rows(noise_ref, out_ref, grid_ref):
     side = noise_ref.shape[0]
     high_rows = grid_ref.shape[0] // side
-    nt = (((1,), (1,)), ((), ()))
     tn = (((0,), (0,)), ((), ()))
-    one, zero = jnp.float32(1), jnp.float32(0)
-
-    @pl.loop(0, side // ROWS_STEP)
-    def _(step):
-        iota_high = lax.broadcasted_iota(jnp.int32, (high_rows, count), 0)
-        iota_low = lax.broadcasted_iota(jnp.int32, (LOW, count), 0)
-        block = pl.ds(pl.multiple_of(step * ROWS_STEP, ROWS_STEP), ROWS_STEP)
-        words = jnp.concatenate([places_ref[d, block, :] for d in range(blocks)], axis=1)
-        locals_ = (words >> 16) - first
-        weights = (words & (SHIFT - 1)).astype(jnp.float32) * (1 / LEVELS) * mass_row[...]
-        for j in range(ROWS_STEP):
-            local = locals_[j : j + 1, :]
-            hot = jnp.where(iota_high == (local >> LOW_BITS), one, zero)
-            low = jnp.where(iota_low == (local & (LOW - 1)), weights[j : j + 1, :], zero)
-            part = lax.dot_general(
-                hot.astype(jnp.bfloat16),
-                low.astype(jnp.bfloat16),
-                nt,
-                preferred_element_type=jnp.float32,
-            )
-            row = pl.multiple_of((step * ROWS_STEP + j) * high_rows, 8)
-            grid_ref[pl.ds(row, high_rows), :LOW] = part
-
     noise = noise_ref[...].astype(jnp.bfloat16)
     for h in range(out_ref.shape[0] // LOW):
         high, low = split(grid_ref[pl.ds(h, side, stride=high_rows), :])
@@ -610,7 +816,9 @@
     posterior = (expo * (jnp.exp(peak_own - peak) / total))[:, :images]
     post_ref[...] = posterior.astype(jnp.bfloat16)
     mass = jnp.sum(posterior, axis=1, keepdims=True)
-    mass_ref[...] = jnp.broadcast_to(mass, (count, LANES)).T[:8, :]
+    mass_t = jnp.broadcast_to(mass, (count, LANES)).T
+    for h in range(count // LANES):
+        mass_ref[h : h + 1, :] = mass_t[:1, h * LANES : (h + 1) * LANES]
 
     for r in range(lines):
         store_copy(r).wait()
@@ -643,7 +851,7 @@
         out_shape=(
             jax.ShapeDtypeStruct((total, pixels), jnp.bfloat16),
             jax.ShapeDtypeStruct((count, total), jnp.bfloat16),
-            jax.ShapeDtypeStruct((8, count), jnp.float32),
+            jax.ShapeDtypeStruct((count // LANES, LANES), jnp.float32),
             jax.ShapeDtypeStruct((side, count), jnp.int32),
             jax.ShapeDtypeStruct((side * count // BATCH, BATCH), jnp.int32),
             jax.ShapeDtypeStruct((8, side), jnp.int32),
@@ -679,7 +887,7 @@
     places = lax.all_gather(words, "orient", axis=0)
     volume = insert_data(post, gathered, interp, voxels, clash, side * side)
     return reduce_rows(
-        volume, mass[0].reshape(-1, LANES), places, inv_noise, groups, orient
+        volume, mass, places, inv_noise, groups, orient
     )
 
 

time: 179 us -> 158 us (0.88)
  the two profiles are of different devices: /device:TPU:13 before, /device:TPU:0 now
where the time goes in v2:
time: 158 us; the launch traced here: 157 us
  Pallas kernels  138 us (87%)
  between operations  14 us (9%)
  local copies, waits for them, and re-layouts  5.44 us (3%)
    pallas_call x1, Pallas kernels, gather_scores(): pl.pallas_call(functools.partial(gather_kernel, orient), out_shape=(jax.S...  52.6 us
    pallas_call x1, Pallas kernels, insert_data(): pl.pallas_call(data_kernel, grid=(steps,), out_shape=jax.ShapeDtypeStruct...  50.2 us
    pallas_call x1, Pallas kernels, reduce_rows(): pl.pallas_call(functools.partial(reduce_kernel, groups, orient), out_shap...  34.9 us
    unnamed x2, local copies, waits for them, and re-layouts  3.34 us
  transfers between devices with their start and end apart: 1, of which 0 were waited for; matrix products, arithmetic and copies ran while one was open for 0% of the time, Pallas kernels for 32%

profile of v2, /device:TPU:0, one launch (start us, length us, event | category | flops | bytes accessed | tf_op | source)
XLA Modules:
  0.0 157.1 jit_solution(17433237158997468432)
XLA Ops:
  7.2 0.0 all-gather.3.cloned.1.call-start
  7.2 2.1 %reshape.13.images_ref = bf16[48,4096]{1,0:T(8,128)(2,1)} reshape(bf16[12,16384]{1,0:T(8,128)(2,1)} %param.5) | data formatting | bytes 786432 | tf_op jit(solution)/shard_map/reshape | solution.py:879
  9.3 52.6 %shard_map.68 = (bf16[192,16384]{1,0:T(8,128)(2,1)}, bf16[256,192]{1,0:T(8,128)(2,1)}, f32[2,128]{1,0:T(2,128)}, s32[128,256]{1,0:T(8,128)}, s32[256,128]{1,0:T(8,128)}, /*index=5*/s32[8,128]{1,0:T(8,128)}) custom-call(bf16[48,4096]{1,0:T(8,128)(2,1)} %reshape.13.images_ref, bf16[256,16384]{1,0:T(8,128)(2,1)} %templates_ref.1, f32[1,16384]{1,0:T(1,128)} %bitcast.5, ...), custom_call_target="tpu_custom_call" | custom-call | tf_op jit(solution)/shard_map/pallas_call | solution.py:849
  61.9 0.0 all-gather.3.cloned.1.call-update
  61.9 50.2 %shard_map.69 = f32[16384,128]{1,0:T(8,128)} custom-call(bf16[256,192]{1,0:T(8,128)(2,1)} %get-tuple-element.8.post_ref, bf16[192,16384]{1,0:T(8,128)(2,1)} %get-tuple-element.9.images_ref, f32[256,128]{1,0:T(8,128)} %interp_ref.3, s32[256,128]{1,0:T(8,128)} %get-tuple-element.10.idx_ref, s32[8,128]{1,0:T(8,128)} %get-tuple-element.11.clash_ref), custom_call_target="tpu_custom_call" | custom-call | flops 199999995904 | bytes 200000000 | tf_op jit(solution)/shard_map/pallas_call | solution.py:104
  112.1 0.0 all-gather.3.cloned.1.call-done
  112.1 34.9 %shard_map.70 = (f32[512,128]{1,0:T(8,128)}, f32[512,128]{1,0:T(8,128)}) custom-call(f32[16,2,512,128]{3,2,1,0:T(8,128)} %bitcast.3, f32[2,128]{1,0:T(2,128)} %get-tuple-element.12.mass_ref, s32[16,128,256]{2,1,0:T(8,128)} %bitcast.4, f32[128,128]{1,0:T(8,128)} %noise_ref.1), custom_call_target="tpu_custom_call" | custom-call | tf_op jit(solution)/shard_map/pallas_call | solution.py:472
  147.0 1.7 %copy.9 = f32[512,128]{1,0:T(8,128)} copy(f32[512,128]{1,0:T(8,128)} %get-tuple-element.16) | data formatting | bytes 524288
  148.6 1.7 %copy.10 = f32[512,128]{1,0:T(8,128)} copy(f32[512,128]{1,0:T(8,128)} %get-tuple-element.17) | data formatting | bytes 524288
Async XLA Ops:
  7.2 104.9 %all-gather.3.cloned.1.call-start = ((), (), s32[]{:S(2)}) async-start(), calls=%async_computation | async-start | bytes 2228224 | tf_op jit(solution)/shard_map/all_gather | solution.py:887
Sparse Core Ops, SparseCore 0:
  62.0 42.0 all-gather.2

commit v3 on v2

--- a/solution.py
+++ b/solution.py
@@ -17,7 +17,7 @@
 NORM_COLS = 1024
 LEVELS = 65535
 SHIFT = 65536
-LOW_BITS = 5
+LOW_BITS = 6
 LOW = 1 << LOW_BITS
 VMEM_LIMIT = 56 * 2**20
 
@@ -148,6 +148,8 @@
     last,
     last_in,
     masses,
+    twin,
+    twin_in,
     own_sem,
     pair_send,
     pair_recv,
@@ -163,6 +165,8 @@
     last_recv,
     mass_send,
     mass_recv,
+    twin_send,
+    twin_recv,
 ):
     lines, across = LINES, orient // (2 * LINES)
     devices = groups * orient
@@ -313,9 +317,16 @@
             for j in reversed(range(across)):
                 pair_copy(k, i, j).start()
 
+    twin_group = group + 1 - 2 * lax.rem(group, 2)
+
+    def mass_sent(s):
+        return lax.rem(lax.div(lax.rem(rank + s, devices), orient), 2) == core
+
     @pl.loop(1, devices)
     def _(s):
-        mass_copy(s).start()
+        @pl.when(mass_sent(s))
+        def _():
+            mass_copy(s).start()
 
     def narrow(value):
         return value.astype(jnp.bfloat16)
@@ -398,7 +409,7 @@
     mass_rows = mass_ref.shape[0]
 
     def add_mass(d, ref):
-        start = lax.rem(d, orient) * (mass_rows * LANES)
+        start = lax.div(lax.rem(d, orient), 2) * (mass_rows * LANES)
         for k in range(mass_rows):
             lanes = pl.ds(pl.multiple_of(start + k * LANES, LANES), LANES)
             mass_row[:, lanes] += ref[k : k + 1, :]
@@ -406,7 +417,9 @@
     steps, slots = noise_ref.shape[0] // ROWS_STEP, 3 * (lines + 2)
 
     def weigh(w):
-        weight_step(w, rank * out_ref.shape[0], places_ref, mass_row, grid_ref)
+        rows = out_ref.shape[0]
+        firsts = (rank * rows, (twin_group * orient + place) * rows)
+        weight_step(w, firsts, places_ref, mass_row, grid_ref)
 
     @pl.loop(0, slots)
     def _(slot):
@@ -426,12 +439,22 @@
 
         @pl.when(slot == 1)
         def _():
-            add_mass(rank, mass_ref)
+            @pl.when(core == lax.rem(group, 2))
+            def _():
+                add_mass(rank, mass_ref)
 
             @pl.loop(1, devices)
             def _(s):
-                mass_copy(s).wait()
-                add_mass(lax.rem(rank + devices - s, devices), masses.at[s])
+                sender = lax.rem(rank + devices - s, devices)
+
+                @pl.when(lax.rem(sender, 2) == lax.rem(group, 2))
+                def _():
+                    mass_copy(s).wait_recv()
+                    add_mass(sender, masses.at[s])
+
+                @pl.when(mass_sent(s))
+                def _():
+                    mass_copy(s).wait_send()
 
         @pl.when((slot >= 2) & (slot < 2 + steps))
         def _():
@@ -441,10 +464,17 @@
     def _(w):
         weigh(w)
 
-    weight_rows(noise_ref, weight_ref, grid_ref)
+    weight_rows(noise_ref, twin, grid_ref, 1)
+    exchange = remote(
+        twin, twin_in, twin_send, twin_recv, twin_group, row, col, core
+    )
+    exchange.start()
+    weight_rows(noise_ref, weight_ref, grid_ref, 0)
     for k in range(lines - 1):
         last_copy(k).wait()
         out_ref[...] += last_in[k].astype(jnp.float32)
+    exchange.wait()
+    weight_ref[...] += twin_in[...].astype(jnp.float32)
 
 
 def reduce_rows(volume, mass_rows, places_t, inv_noise, groups, orient):
@@ -482,14 +512,16 @@
             pl.BlockSpec(memory_space=pltpu.VMEM),
         ),
         scratch_shapes=[
-            pltpu.VMEM((side * max(8, rows // LOW), LANES), jnp.float32),
+            pltpu.VMEM((2 * side * max(8, rows // LOW), LANES), jnp.float32),
             pltpu.VMEM((1, places_t.shape[0] * places_t.shape[2]), jnp.float32),
         ]
         + [pltpu.VMEM(parts, jnp.float32)] * 2
         + [pltpu.VMEM(s, jnp.bfloat16) for s in shapes for _ in range(2)]
         + [pltpu.VMEM(masses, jnp.float32)]
+        + [pltpu.VMEM((rows, side), jnp.bfloat16)] * 2
         + [pltpu.SemaphoreType.DMA((lines, groups * across))] * 3
-        + [pltpu.SemaphoreType.DMA(s) for s in sems for _ in range(2)],
+        + [pltpu.SemaphoreType.DMA(s) for s in sems for _ in range(2)]
+        + [pltpu.SemaphoreType.DMA] * 2,
         compiler_params=pltpu.CompilerParams(
             collective_id=0, has_side_effects=True, vmem_limit_bytes=VMEM_LIMIT
         ),
@@ -501,20 +533,26 @@
     return high, (value - high.astype(jnp.float32)).astype(jnp.bfloat16)
 
 
-def weight_step(step, first, places_ref, mass_row, grid_ref):
+def weight_step(step, firsts, places_ref, mass_row, grid_ref):
     blocks, side, each = places_ref.shape
     count = blocks * each
     high_rows = grid_ref.shape[0] // side
     nt = (((1,), (1,)), ((), ()))
     one, zero = jnp.float32(1), jnp.float32(0)
-    iota_high = lax.broadcasted_iota(jnp.int32, (high_rows, count), 0)
+    spot = lax.broadcasted_iota(jnp.int32, (high_rows, count), 0)
+    each_high = high_rows // 2
+    iota_high = jnp.where(
+        spot < each_high,
+        (firsts[0] >> LOW_BITS) + spot,
+        (firsts[1] >> LOW_BITS) + spot - each_high,
+    )
     iota_low = lax.broadcasted_iota(jnp.int32, (LOW, count), 0)
     block = pl.ds(pl.multiple_of(step * ROWS_STEP, ROWS_STEP), ROWS_STEP)
     words = jnp.concatenate([places_ref[d, block, :] for d in range(blocks)], axis=1)
-    locals_ = (words >> 16) - first
+    voxels = words >> 16
     weights = (words & (SHIFT - 1)).astype(jnp.float32) * (1 / LEVELS) * mass_row[...]
     for j in range(ROWS_STEP):
-        local = locals_[j : j + 1, :]
+        local = voxels[j : j + 1, :]
         hot = jnp.where(iota_high == (local >> LOW_BITS), one, zero)
         low = jnp.where(iota_low == (local & (LOW - 1)), weights[j : j + 1, :], zero)
         part = lax.dot_general(
@@ -527,22 +565,23 @@
         grid_ref[pl.ds(row, high_rows), :LOW] = part
 
 
-def weight_rows(noise_ref, out_ref, grid_ref):
+def weight_rows(noise_ref, out_ref, grid_ref, part):
     side = noise_ref.shape[0]
     high_rows = grid_ref.shape[0] // side
     tn = (((0,), (0,)), ((), ()))
     noise = noise_ref[...].astype(jnp.bfloat16)
     for h in range(out_ref.shape[0] // LOW):
-        high, low = split(grid_ref[pl.ds(h, side, stride=high_rows), :])
+        first = part * (high_rows // 2) + h
+        high, low = split(grid_ref[pl.ds(first, side, stride=high_rows), :])
         block = lax.dot_general(
             high, noise, tn, preferred_element_type=jnp.float32
         ) + lax.dot_general(low, noise, tn, preferred_element_type=jnp.float32)
-        out_ref[h * LOW : (h + 1) * LOW, :] = block[:LOW]
+        out_ref[h * LOW : (h + 1) * LOW, :] = block[:LOW].astype(out_ref.dtype)
 
 
 def gather_kernel(
     orient,
-    images_ref,
+    own_ref,
     templates_ref,
     noise_ref,
     index_ref,
@@ -550,9 +589,13 @@
     gathered_ref,
     post_ref,
     mass_ref,
-    words_ref,
+    places_ref,
     rows_ref,
     clash_ref,
+    images_ref,
+    wide,
+    words,
+    words_in,
     raw,
     weighted,
     whole,
@@ -566,6 +609,8 @@
     recv_sem,
     stat_send,
     stat_recv,
+    word_send,
+    word_recv,
 ):
     lines, across = LINES, orient // (2 * LINES)
     group, place = lax.axis_index("dp"), lax.axis_index("orient")
@@ -603,6 +648,12 @@
     for k in range(fold):
         load_copy(k).start()
 
+    own_rows = own_ref.shape[0]
+    for k in range(fold):
+        wide[k * own_rows : (k + 1) * own_rows, :] = own_ref[
+            :, k * width : (k + 1) * width
+        ].astype(jnp.float32)
+    images_ref[...] = wide[...].astype(jnp.bfloat16)
     pl.semaphore_wait(barrier, orient - 1)
 
     def copy(source, r, q, s, way, target):
@@ -677,7 +728,44 @@
             :, h * BATCH : (h + 1) * BATCH
         ]
     level = (interp_ref[...] * LEVELS + 0.5).astype(jnp.int32)
-    words_ref[...] = (index * SHIFT + level).T
+    words[...] = (index * SHIFT + level).T
+
+    bearer = lax.rem(group, 2) == core
+
+    def word_copy(source, r, q, way, target):
+        slot = r * across + q
+        return pltpu.make_async_remote_copy(
+            src_ref=words if source is None else words_in.at[slot],
+            dst_ref=words_in.at[slot],
+            send_sem=word_send.at[slot, way],
+            recv_sem=word_recv.at[slot],
+            device_id=(group, target),
+            device_id_type=mesh_ids,
+        )
+
+    def word_arrived(r, q):
+        word_copy(words_in, r, q, 0, place + 1 - 2 * core).wait_recv()
+
+    def each_word(r, q, act, source=words_in):
+        for way, step in ((0, 1), (1, -1)):
+            onward = row + step
+            along = (onward >= 0) & (onward < lines)
+            if source is not None:
+                along = (q == col) & along & ((row - r) * step > 0)
+
+            @pl.when(along)
+            def _(way=way, onward=onward):
+                act(word_copy(source, r, q, way, at(onward, col, core)))
+
+        for way, step in ((2, 1), (3, -1)):
+            onward = col + step
+            beside = (onward >= 0) & (onward < across) & ((col - q) * step >= 0)
+
+            @pl.when(beside)
+            def _(way=way, onward=onward):
+                act(word_copy(source, r, q, way, at(row, onward, core)))
+
+        act(word_copy(source, r, q, 4, place + 1 - 2 * core))
 
     def weigh(k):
         load_copy(k).wait()
@@ -705,7 +793,8 @@
         total = 2 * across * block_rows
         out_row = lax.broadcasted_iota(jnp.int32, (total, total), 0)
         from_row = lax.broadcasted_iota(jnp.int32, (total, total), 1)
-        wanted = (out_row % line_images) * fold + out_row // line_images
+        image, piece = out_row % line_images, out_row // line_images
+        wanted = (image // own_rows) * block_rows + piece * own_rows + image % own_rows
         pick = jnp.where(from_row == wanted, 1.0, 0.0).astype(jnp.bfloat16)
         sorted_ = jnp.dot(pick, block, preferred_element_type=jnp.float32)
         sorted_ = sorted_.astype(jnp.bfloat16)
@@ -765,6 +854,18 @@
             def _(j):
                 weigh(s * (fold // PARTS) + j)
 
+        @pl.when(bearer & (n == lines) & (s == 0))
+        def _():
+            each_word(row, col, lambda c: c.start(), None)
+
+        for sign in (1, -1):
+            r = row + sign * s
+
+            @pl.when(bearer & (n == lines) & (s > 0) & (r >= 0) & (r < lines))
+            def _(r=r):
+                word_arrived(r, col)
+                each_word(r, col, lambda c: c.start())
+
         last = jnp.maximum(k - 1, 0)
         m, t = lax.div(last, PARTS) + 1, lax.rem(last, PARTS)
 
@@ -802,6 +903,21 @@
         stat_copy(s).start()
 
     landed[0] = stats[...]
+
+    @pl.when(bearer)
+    def _():
+        for e in range(1, across):
+            for side in (1, -1):
+                for d in range(lines):
+                    for sign in (1, -1) if d else (1,):
+                        r, q = row + sign * d, col + side * e
+
+                        @pl.when((r >= 0) & (r < lines) & (q >= 0) & (q < across))
+                        def _(r=r, q=q):
+                            word_arrived(r, q)
+                            each_word(r, q, lambda c: c.start())
+
+        words_in[row * across + col] = words[...]
 
     @pl.loop(1, orient)
     def _(s):
@@ -819,6 +935,24 @@
     mass_t = jnp.broadcast_to(mass, (count, LANES)).T
     for h in range(count // LANES):
         mass_ref[h : h + 1, :] = mass_t[:1, h * LANES : (h + 1) * LANES]
+
+    @pl.when(jnp.logical_not(bearer))
+    def _():
+        for r in range(lines):
+            for q in range(across):
+                word_arrived(r, q)
+
+    places_ref[...] = words_in[...]
+
+    @pl.when(bearer)
+    def _():
+        each_word(row, col, lambda c: c.wait_send(), None)
+        for r in range(lines):
+            for q in range(across):
+
+                @pl.when((row != r) | (col != q))
+                def _(r=r, q=q):
+                    each_word(r, q, lambda c: c.wait_send())
 
     for r in range(lines):
         store_copy(r).wait()
@@ -852,13 +986,17 @@
             jax.ShapeDtypeStruct((total, pixels), jnp.bfloat16),
             jax.ShapeDtypeStruct((count, total), jnp.bfloat16),
             jax.ShapeDtypeStruct((count // LANES, LANES), jnp.float32),
-            jax.ShapeDtypeStruct((side, count), jnp.int32),
+            jax.ShapeDtypeStruct((chips, side, count), jnp.int32),
             jax.ShapeDtypeStruct((side * count // BATCH, BATCH), jnp.int32),
             jax.ShapeDtypeStruct((8, side), jnp.int32),
         ),
         in_specs=[vmem, hbm, vmem, vmem, vmem],
         out_specs=(hbm, vmem, vmem, vmem, vmem, vmem),
         scratch_shapes=[
+            pltpu.VMEM((own * fold, width), jnp.bfloat16),
+            pltpu.VMEM((own * fold, width), jnp.float32),
+            pltpu.VMEM((side, count), jnp.int32),
+            pltpu.VMEM((chips, side, count), jnp.int32),
             pltpu.VMEM((orient, own * fold, width), jnp.bfloat16),
             pltpu.VMEM((count, pixels), jnp.bfloat16),
             pltpu.VMEM((total, pixels), jnp.bfloat16),
@@ -872,19 +1010,20 @@
             pltpu.SemaphoreType.DMA((orient, PARTS)),
             pltpu.SemaphoreType.DMA((orient,)),
             pltpu.SemaphoreType.DMA((orient,)),
+            pltpu.SemaphoreType.DMA((chips, 5)),
+            pltpu.SemaphoreType.DMA((chips,)),
         ],
         compiler_params=pltpu.CompilerParams(
             collective_id=1, has_side_effects=True, vmem_limit_bytes=VMEM_LIMIT
         ),
-    )(images.reshape(own * fold, width), templates, noise_flat, index, interp)
+    )(images, templates, noise_flat, index, interp)
 
 
 def shards(groups, orient, images, templates, index, interp, inv_noise):
     side = inv_noise.shape[0]
-    gathered, post, mass, words, voxels, clash = gather_scores(
+    gathered, post, mass, places, voxels, clash = gather_scores(
         images, templates, index, interp, inv_noise.reshape(1, -1), orient
     )
-    places = lax.all_gather(words, "orient", axis=0)
     volume = insert_data(post, gathered, interp, voxels, clash, side * side)
     return reduce_rows(
         volume, mass, places, inv_noise, groups, orient

time: 158 us -> 156 us (0.987)
  Pallas kernels: 138 us -> 152 us
  between operations: 14 us -> 0.65 us
  local copies, waits for them, and re-layouts: 5.44 us -> 3.34 us
    pallas_call x1, Pallas kernels: 52.6 us -> 66.5 us  [gather_scores(): pl.pallas_call(functools.partial(gather_kernel, orient), out_shape=(jax.S...]
    reshape x1 -> x0, local copies, waits for them, and re-layouts: 2.1 us -> none  [gather_scores(): images.reshape(own * fold, width)]
  transfers between devices with their start and end apart: 1 -> 0, of which waited for: 0 -> 0; matrix products, arithmetic and copies ran while one was open for 0% -> 0% of each run, Pallas kernels for 32% -> 0%
where the time goes in v3:
time: 156 us
  Pallas kernels  152 us (97%)
  local copies, waits for them, and re-layouts  3.34 us (2%)
    pallas_call x1, Pallas kernels, gather_scores(): pl.pallas_call(functools.partial(gather_kernel, orient), out_shape=(jax.S...  66.5 us
    pallas_call x1, Pallas kernels, insert_data(): pl.pallas_call(data_kernel, grid=(steps,), out_shape=jax.ShapeDtypeStruct...  50.6 us
    pallas_call x1, Pallas kernels, reduce_rows(): pl.pallas_call(functools.partial(reduce_kernel, groups, orient), out_shap...  34.7 us
    unnamed x2, local copies, waits for them, and re-layouts  3.34 us

profile of v3, /device:TPU:0, one launch (start us, length us, event | category | flops | bytes accessed | tf_op | source)
XLA Modules:
  0.0 155.8 jit_solution(3913143797709697683)
XLA Ops:
  0.6 66.5 %shard_map.68 = (bf16[192,16384]{1,0:T(8,128)(2,1)}, bf16[256,192]{1,0:T(8,128)(2,1)}, f32[2,128]{1,0:T(2,128)}, s32[8,128,256]{2,1,0:T(8,128)}, s32[256,128]{1,0:T(8,128)}, /*index=5*/s32[8,128]{1,0:T(8,128)}) custom-call(bf16[12,16384]{1,0:T(8,128)(2,1)} %own_ref.1, bf16[256,16384]{1,0:T(8,128)(2,1)} %templates_ref.1, f32[1,16384]{1,0:T(1,128)} %bitcast.3, ...), custom_call_target="tpu_custom_call" | custom-call | tf_op jit(solution)/shard_map/pallas_call | solution.py:983
  67.2 50.6 %shard_map.69 = f32[16384,128]{1,0:T(8,128)} custom-call(bf16[256,192]{1,0:T(8,128)(2,1)} %get-tuple-element.8.post_ref, bf16[192,16384]{1,0:T(8,128)(2,1)} %get-tuple-element.9.images_ref, f32[256,128]{1,0:T(8,128)} %interp_ref.3, s32[256,128]{1,0:T(8,128)} %get-tuple-element.10.idx_ref, s32[8,128]{1,0:T(8,128)} %get-tuple-element.11.clash_ref), custom_call_target="tpu_custom_call" | custom-call | flops 199999995904 | bytes 200000000 | tf_op jit(solution)/shard_map/pallas_call | solution.py:104
  117.8 34.7 %shard_map.70 = (f32[512,128]{1,0:T(8,128)}, f32[512,128]{1,0:T(8,128)}) custom-call(f32[16,2,512,128]{3,2,1,0:T(8,128)} %bitcast.2, f32[2,128]{1,0:T(2,128)} %get-tuple-element.12.mass_ref, s32[8,128,256]{2,1,0:T(8,128)} %get-tuple-element.13.places_ref, f32[128,128]{1,0:T(8,128)} %noise_ref.1), custom_call_target="tpu_custom_call" | custom-call | tf_op jit(solution)/shard_map/pallas_call | solution.py:502
  152.5 1.7 %copy.9 = f32[512,128]{1,0:T(8,128)} copy(f32[512,128]{1,0:T(8,128)} %get-tuple-element.16) | data formatting | bytes 524288
  154.1 1.7 %copy.10 = f32[512,128]{1,0:T(8,128)} copy(f32[512,128]{1,0:T(8,128)} %get-tuple-element.17) | data formatting | bytes 524288

commit v4 on v3

--- a/solution.py
+++ b/solution.py
@@ -319,8 +319,12 @@
 
     twin_group = group + 1 - 2 * lax.rem(group, 2)
 
+    def column(d):
+        return lax.rem(lax.div(lax.rem(d, orient), 2), across)
+
     def mass_sent(s):
-        return lax.rem(lax.div(lax.rem(rank + s, devices), orient), 2) == core
+        target = lax.rem(rank + s, devices)
+        return (lax.rem(lax.div(target, orient), 2) == core) & (column(target) == col)
 
     @pl.loop(1, devices)
     def _(s):
@@ -409,7 +413,7 @@
     mass_rows = mass_ref.shape[0]
 
     def add_mass(d, ref):
-        start = lax.div(lax.rem(d, orient), 2) * (mass_rows * LANES)
+        start = lax.div(lax.rem(d, orient), 2 * across) * (mass_rows * LANES)
         for k in range(mass_rows):
             lanes = pl.ds(pl.multiple_of(start + k * LANES, LANES), LANES)
             mass_row[:, lanes] += ref[k : k + 1, :]
@@ -418,8 +422,24 @@
 
     def weigh(w):
         rows = out_ref.shape[0]
-        firsts = (rank * rows, (twin_group * orient + place) * rows)
+        firsts = [
+            (x * orient + (row * across + col_at(j)) * 2 + core) * rows
+            for x in (group, twin_group)
+            for j in range(across)
+        ]
         weight_step(w, firsts, places_ref, mass_row, grid_ref)
+
+    def twin_copy(n):
+        return remote(
+            twin.at[n - 1],
+            twin_in.at[n - 1],
+            twin_send.at[n - 1],
+            twin_recv.at[n - 1],
+            (group, twin_group)[n // across],
+            row,
+            col_at(n % across),
+            core,
+        )
 
     @pl.loop(0, slots)
     def _(slot):
@@ -447,7 +467,7 @@
             def _(s):
                 sender = lax.rem(rank + devices - s, devices)
 
-                @pl.when(lax.rem(sender, 2) == lax.rem(group, 2))
+                @pl.when((lax.rem(sender, 2) == lax.rem(group, 2)) & (column(sender) == col))
                 def _():
                     mass_copy(s).wait_recv()
                     add_mass(sender, masses.at[s])
@@ -456,25 +476,24 @@
                 def _():
                     mass_copy(s).wait_send()
 
-        @pl.when((slot >= 2) & (slot < 2 + steps))
-        def _():
-            weigh(slot - 2)
-
-    @pl.loop(slots - 2, max(steps, slots - 2))
-    def _(w):
-        weigh(w)
-
-    weight_rows(noise_ref, twin, grid_ref, 1)
-    exchange = remote(
-        twin, twin_in, twin_send, twin_recv, twin_group, row, col, core
-    )
-    exchange.start()
-    weight_rows(noise_ref, weight_ref, grid_ref, 0)
+        @pl.when((slot >= 2) & (slot < 2 + steps // 2))
+        def _():
+            weigh(2 * slot - 4)
+            weigh(2 * slot - 3)
+
+        @pl.when(slot == 2 + steps // 2)
+        def _():
+            for n in range(1, 2 * across):
+                weight_rows(noise_ref, twin.at[n - 1], grid_ref, n, 2 * across)
+                twin_copy(n).start()
+
+    weight_rows(noise_ref, weight_ref, grid_ref, 0, 2 * across)
+    for n in range(1, 2 * across):
+        twin_copy(n).wait()
+        weight_ref[...] += twin_in[n - 1].astype(jnp.float32)
     for k in range(lines - 1):
         last_copy(k).wait()
         out_ref[...] += last_in[k].astype(jnp.float32)
-    exchange.wait()
-    weight_ref[...] += twin_in[...].astype(jnp.float32)
 
 
 def reduce_rows(volume, mass_rows, places_t, inv_noise, groups, orient):
@@ -512,25 +531,20 @@
             pl.BlockSpec(memory_space=pltpu.VMEM),
         ),
         scratch_shapes=[
-            pltpu.VMEM((2 * side * max(8, rows // LOW), LANES), jnp.float32),
+            pltpu.VMEM((2 * across * side * max(8, rows // LOW), LANES), jnp.float32),
             pltpu.VMEM((1, places_t.shape[0] * places_t.shape[2]), jnp.float32),
         ]
         + [pltpu.VMEM(parts, jnp.float32)] * 2
         + [pltpu.VMEM(s, jnp.bfloat16) for s in shapes for _ in range(2)]
         + [pltpu.VMEM(masses, jnp.float32)]
-        + [pltpu.VMEM((rows, side), jnp.bfloat16)] * 2
+        + [pltpu.VMEM((2 * across - 1, rows, side), jnp.bfloat16)] * 2
         + [pltpu.SemaphoreType.DMA((lines, groups * across))] * 3
         + [pltpu.SemaphoreType.DMA(s) for s in sems for _ in range(2)]
-        + [pltpu.SemaphoreType.DMA] * 2,
+        + [pltpu.SemaphoreType.DMA((2 * across - 1,))] * 2,
         compiler_params=pltpu.CompilerParams(
             collective_id=0, has_side_effects=True, vmem_limit_bytes=VMEM_LIMIT
         ),
     )(volume.reshape(chips, 2, rows, side), mass_rows, places_t, inv_noise)
-
-
-def split(value):
-    high = value.astype(jnp.bfloat16)
-    return high, (value - high.astype(jnp.float32)).astype(jnp.bfloat16)
 
 
 def weight_step(step, firsts, places_ref, mass_row, grid_ref):
@@ -540,12 +554,11 @@
     nt = (((1,), (1,)), ((), ()))
     one, zero = jnp.float32(1), jnp.float32(0)
     spot = lax.broadcasted_iota(jnp.int32, (high_rows, count), 0)
-    each_high = high_rows // 2
-    iota_high = jnp.where(
-        spot < each_high,
-        (firsts[0] >> LOW_BITS) + spot,
-        (firsts[1] >> LOW_BITS) + spot - each_high,
-    )
+    each_high = high_rows // len(firsts)
+    iota_high = spot
+    for n, first in enumerate(firsts):
+        shift = lax.div(first, LOW) - n * each_high
+        iota_high = jnp.where(spot // each_high == n, spot + shift, iota_high)
     iota_low = lax.broadcasted_iota(jnp.int32, (LOW, count), 0)
     block = pl.ds(pl.multiple_of(step * ROWS_STEP, ROWS_STEP), ROWS_STEP)
     words = jnp.concatenate([places_ref[d, block, :] for d in range(blocks)], axis=1)
@@ -565,17 +578,18 @@
         grid_ref[pl.ds(row, high_rows), :LOW] = part
 
 
-def weight_rows(noise_ref, out_ref, grid_ref, part):
+def weight_rows(noise_ref, out_ref, grid_ref, part, ranges):
     side = noise_ref.shape[0]
     high_rows = grid_ref.shape[0] // side
-    tn = (((0,), (0,)), ((), ()))
     noise = noise_ref[...].astype(jnp.bfloat16)
     for h in range(out_ref.shape[0] // LOW):
-        first = part * (high_rows // 2) + h
-        high, low = split(grid_ref[pl.ds(first, side, stride=high_rows), :])
+        first = part * (high_rows // ranges) + h
         block = lax.dot_general(
-            high, noise, tn, preferred_element_type=jnp.float32
-        ) + lax.dot_general(low, noise, tn, preferred_element_type=jnp.float32)
+            grid_ref[pl.ds(first, side, stride=high_rows), :].astype(jnp.bfloat16),
+            noise,
+            (((0,), (0,)), ((), ())),
+            preferred_element_type=jnp.float32,
+        )
         out_ref[h * LOW : (h + 1) * LOW, :] = block[:LOW].astype(out_ref.dtype)
 
 
@@ -732,40 +746,31 @@
 
     bearer = lax.rem(group, 2) == core
 
-    def word_copy(source, r, q, way, target):
-        slot = r * across + q
+    def word_copy(source, r, way, target):
         return pltpu.make_async_remote_copy(
-            src_ref=words if source is None else words_in.at[slot],
-            dst_ref=words_in.at[slot],
-            send_sem=word_send.at[slot, way],
-            recv_sem=word_recv.at[slot],
+            src_ref=words if source is None else words_in.at[r],
+            dst_ref=words_in.at[r],
+            send_sem=word_send.at[r, way],
+            recv_sem=word_recv.at[r],
             device_id=(group, target),
             device_id_type=mesh_ids,
         )
 
-    def word_arrived(r, q):
-        word_copy(words_in, r, q, 0, place + 1 - 2 * core).wait_recv()
-
-    def each_word(r, q, act, source=words_in):
+    def word_arrived(r):
+        word_copy(words_in, r, 2, place + 1 - 2 * core).wait_recv()
+
+    def each_word(r, act, source=words_in):
         for way, step in ((0, 1), (1, -1)):
             onward = row + step
             along = (onward >= 0) & (onward < lines)
             if source is not None:
-                along = (q == col) & along & ((row - r) * step > 0)
+                along = along & ((row - r) * step > 0)
 
             @pl.when(along)
             def _(way=way, onward=onward):
-                act(word_copy(source, r, q, way, at(onward, col, core)))
-
-        for way, step in ((2, 1), (3, -1)):
-            onward = col + step
-            beside = (onward >= 0) & (onward < across) & ((col - q) * step >= 0)
-
-            @pl.when(beside)
-            def _(way=way, onward=onward):
-                act(word_copy(source, r, q, way, at(row, onward, core)))
-
-        act(word_copy(source, r, q, 4, place + 1 - 2 * core))
+                act(word_copy(source, r, way, at(onward, col, core)))
+
+        act(word_copy(source, r, 2, place + 1 - 2 * core))
 
     def weigh(k):
         load_copy(k).wait()
@@ -856,15 +861,15 @@
 
         @pl.when(bearer & (n == lines) & (s == 0))
         def _():
-            each_word(row, col, lambda c: c.start(), None)
+            each_word(row, lambda c: c.start(), None)
 
         for sign in (1, -1):
             r = row + sign * s
 
             @pl.when(bearer & (n == lines) & (s > 0) & (r >= 0) & (r < lines))
             def _(r=r):
-                word_arrived(r, col)
-                each_word(r, col, lambda c: c.start())
+                word_arrived(r)
+                each_word(r, lambda c: c.start())
 
         last = jnp.maximum(k - 1, 0)
         m, t = lax.div(last, PARTS) + 1, lax.rem(last, PARTS)
@@ -906,18 +911,7 @@
 
     @pl.when(bearer)
     def _():
-        for e in range(1, across):
-            for side in (1, -1):
-                for d in range(lines):
-                    for sign in (1, -1) if d else (1,):
-                        r, q = row + sign * d, col + side * e
-
-                        @pl.when((r >= 0) & (r < lines) & (q >= 0) & (q < across))
-                        def _(r=r, q=q):
-                            word_arrived(r, q)
-                            each_word(r, q, lambda c: c.start())
-
-        words_in[row * across + col] = words[...]
+        words_in[row] = words[...]
 
     @pl.loop(1, orient)
     def _(s):
@@ -939,20 +933,18 @@
     @pl.when(jnp.logical_not(bearer))
     def _():
         for r in range(lines):
-            for q in range(across):
-                word_arrived(r, q)
+            word_arrived(r)
 
     places_ref[...] = words_in[...]
 
     @pl.when(bearer)
     def _():
-        each_word(row, col, lambda c: c.wait_send(), None)
+        each_word(row, lambda c: c.wait_send(), None)
         for r in range(lines):
-            for q in range(across):
-
-                @pl.when((row != r) | (col != q))
-                def _(r=r, q=q):
-                    each_word(r, q, lambda c: c.wait_send())
+
+            @pl.when(row != r)
+            def _(r=r):
+                each_word(r, lambda c: c.wait_send())
 
     for r in range(lines):
         store_copy(r).wait()
@@ -986,7 +978,7 @@
             jax.ShapeDtypeStruct((total, pixels), jnp.bfloat16),
             jax.ShapeDtypeStruct((count, total), jnp.bfloat16),
             jax.ShapeDtypeStruct((count // LANES, LANES), jnp.float32),
-            jax.ShapeDtypeStruct((chips, side, count), jnp.int32),
+            jax.ShapeDtypeStruct((LINES, side, count), jnp.int32),
             jax.ShapeDtypeStruct((side * count // BATCH, BATCH), jnp.int32),
             jax.ShapeDtypeStruct((8, side), jnp.int32),
         ),
@@ -996,7 +988,7 @@
             pltpu.VMEM((own * fold, width), jnp.bfloat16),
             pltpu.VMEM((own * fold, width), jnp.float32),
             pltpu.VMEM((side, count), jnp.int32),
-            pltpu.VMEM((chips, side, count), jnp.int32),
+            pltpu.VMEM((LINES, side, count), jnp.int32),
             pltpu.VMEM((orient, own * fold, width), jnp.bfloat16),
             pltpu.VMEM((count, pixels), jnp.bfloat16),
             pltpu.VMEM((total, pixels), jnp.bfloat16),
@@ -1010,8 +1002,8 @@
             pltpu.SemaphoreType.DMA((orient, PARTS)),
             pltpu.SemaphoreType.DMA((orient,)),
             pltpu.SemaphoreType.DMA((orient,)),
-            pltpu.SemaphoreType.DMA((chips, 5)),
-            pltpu.SemaphoreType.DMA((chips,)),
+            pltpu.SemaphoreType.DMA((LINES, 3)),
+            pltpu.SemaphoreType.DMA((LINES,)),
         ],
         compiler_params=pltpu.CompilerParams(
             collective_id=1, has_side_effects=True, vmem_limit_bytes=VMEM_LIMIT

time: 156 us -> 155 us (level)
  Pallas kernels: 152 us -> 150 us
where the time goes in v4:
time: 155 us; the launch traced here: 154 us
  Pallas kernels  150 us (97%)
  local copies, waits for them, and re-layouts  3.34 us (2%)
    pallas_call x1, Pallas kernels, gather_scores(): pl.pallas_call(functools.partial(gather_kernel, orient), out_shape=(jax.S...  66.2 us
    pallas_call x1, Pallas kernels, insert_data(): pl.pallas_call(data_kernel, grid=(steps,), out_shape=jax.ShapeDtypeStruct...  50.1 us
    pallas_call x1, Pallas kernels, reduce_rows(): pl.pallas_call(functools.partial(reduce_kernel, groups, orient), out_shap...  34.2 us
    unnamed x2, local copies, waits for them, and re-layouts  3.34 us

profile of v4, /device:TPU:0, one launch (start us, length us, event | category | flops | bytes accessed | tf_op | source)
XLA Modules:
  0.0 154.5 jit_solution(12776671940805128071)
XLA Ops:
  0.6 66.2 %shard_map.68 = (bf16[192,16384]{1,0:T(8,128)(2,1)}, bf16[256,192]{1,0:T(8,128)(2,1)}, f32[2,128]{1,0:T(2,128)}, s32[4,128,256]{2,1,0:T(8,128)}, s32[256,128]{1,0:T(8,128)}, /*index=5*/s32[8,128]{1,0:T(8,128)}) custom-call(bf16[12,16384]{1,0:T(8,128)(2,1)} %own_ref.1, bf16[256,16384]{1,0:T(8,128)(2,1)} %templates_ref.1, f32[1,16384]{1,0:T(1,128)} %bitcast.3, ...), custom_call_target="tpu_custom_call" | custom-call | tf_op jit(solution)/shard_map/pallas_call | solution.py:975
  66.8 50.1 %shard_map.69 = f32[16384,128]{1,0:T(8,128)} custom-call(bf16[256,192]{1,0:T(8,128)(2,1)} %get-tuple-element.8.post_ref, bf16[192,16384]{1,0:T(8,128)(2,1)} %get-tuple-element.9.images_ref, f32[256,128]{1,0:T(8,128)} %interp_ref.3, s32[256,128]{1,0:T(8,128)} %get-tuple-element.10.idx_ref, s32[8,128]{1,0:T(8,128)} %get-tuple-element.11.clash_ref), custom_call_target="tpu_custom_call" | custom-call | flops 199999995904 | bytes 200000000 | tf_op jit(solution)/shard_map/pallas_call | solution.py:104
  116.9 34.2 %shard_map.70 = (f32[512,128]{1,0:T(8,128)}, f32[512,128]{1,0:T(8,128)}) custom-call(f32[16,2,512,128]{3,2,1,0:T(8,128)} %bitcast.2, f32[2,128]{1,0:T(2,128)} %get-tuple-element.12.mass_ref, s32[4,128,256]{2,1,0:T(8,128)} %get-tuple-element.13.places_ref, f32[128,128]{1,0:T(8,128)} %noise_ref.1), custom_call_target="tpu_custom_call" | custom-call | tf_op jit(solution)/shard_map/pallas_call | solution.py:521
  151.1 1.7 %copy.9 = f32[512,128]{1,0:T(8,128)} copy(f32[512,128]{1,0:T(8,128)} %get-tuple-element.16) | data formatting | bytes 524288
  152.8 1.7 %copy.10 = f32[512,128]{1,0:T(8,128)} copy(f32[512,128]{1,0:T(8,128)} %get-tuple-element.17) | data formatting | bytes 524288

commit v5 on v4

--- a/solution.py
+++ b/solution.py
@@ -668,7 +668,57 @@
             :, k * width : (k + 1) * width
         ].astype(jnp.float32)
     images_ref[...] = wide[...].astype(jnp.bfloat16)
+    index = index_ref[...]
+    near = jnp.zeros(index.shape, jnp.int32)
+    spot = lax.broadcasted_iota(jnp.int32, index.shape, 0) % SUB
+    for d in range(1, SUB):
+        same = (index == pltpu.roll(index, d, axis=0)) & (spot >= d)
+        near = near | same.astype(jnp.int32)
+    clash_ref[...] = jnp.zeros_like(clash_ref)
+    for h in range(count // BATCH):
+        clash_ref[h : h + 1, :] = jnp.max(
+            near[h * BATCH : (h + 1) * BATCH, :], axis=0, keepdims=True
+        )
+    index_t = index.T
+    for h in range(count // BATCH):
+        rows_ref[pl.ds(h, index_t.shape[0], stride=count // BATCH), :] = index_t[
+            :, h * BATCH : (h + 1) * BATCH
+        ]
+    level = (interp_ref[...] * LEVELS + 0.5).astype(jnp.int32)
+    words[...] = (index * SHIFT + level).T
     pl.semaphore_wait(barrier, orient - 1)
+
+    bearer = lax.rem(group, 2) == core
+
+    def word_copy(source, r, way, target):
+        return pltpu.make_async_remote_copy(
+            src_ref=words if source is None else words_in.at[r],
+            dst_ref=words_in.at[r],
+            send_sem=word_send.at[r, way],
+            recv_sem=word_recv.at[r],
+            device_id=(group, target),
+            device_id_type=mesh_ids,
+        )
+
+    def word_arrived(r):
+        word_copy(words_in, r, 2, place + 1 - 2 * core).wait_recv()
+
+    def each_word(r, act, source=words_in):
+        for way, step in ((0, 1), (1, -1)):
+            onward = row + step
+            along = (onward >= 0) & (onward < lines)
+            if source is not None:
+                along = along & ((row - r) * step > 0)
+
+            @pl.when(along)
+            def _(way=way, onward=onward):
+                act(word_copy(source, r, way, at(onward, col, core)))
+
+        act(word_copy(source, r, 2, place + 1 - 2 * core))
+
+    @pl.when(bearer)
+    def _():
+        each_word(row, lambda c: c.start(), None)
 
     def copy(source, r, q, s, way, target):
         cols = pl.ds(pl.multiple_of(s * part, part), part)
@@ -724,53 +774,6 @@
     raw[place] = images_ref[...]
     scores[...] = jnp.zeros_like(scores)
     norms[...] = jnp.zeros_like(norms)
-
-    index = index_ref[...]
-    near = jnp.zeros(index.shape, jnp.int32)
-    spot = lax.broadcasted_iota(jnp.int32, index.shape, 0) % SUB
-    for d in range(1, SUB):
-        same = (index == pltpu.roll(index, d, axis=0)) & (spot >= d)
-        near = near | same.astype(jnp.int32)
-    clash_ref[...] = jnp.zeros_like(clash_ref)
-    for h in range(count // BATCH):
-        clash_ref[h : h + 1, :] = jnp.max(
-            near[h * BATCH : (h + 1) * BATCH, :], axis=0, keepdims=True
-        )
-    index_t = index.T
-    for h in range(count // BATCH):
-        rows_ref[pl.ds(h, index_t.shape[0], stride=count // BATCH), :] = index_t[
-            :, h * BATCH : (h + 1) * BATCH
-        ]
-    level = (interp_ref[...] * LEVELS + 0.5).astype(jnp.int32)
-    words[...] = (index * SHIFT + level).T
-
-    bearer = lax.rem(group, 2) == core
-
-    def word_copy(source, r, way, target):
-        return pltpu.make_async_remote_copy(
-            src_ref=words if source is None else words_in.at[r],
-            dst_ref=words_in.at[r],
-            send_sem=word_send.at[r, way],
-            recv_sem=word_recv.at[r],
-            device_id=(group, target),
-            device_id_type=mesh_ids,
-        )
-
-    def word_arrived(r):
-        word_copy(words_in, r, 2, place + 1 - 2 * core).wait_recv()
-
-    def each_word(r, act, source=words_in):
-        for way, step in ((0, 1), (1, -1)):
-            onward = row + step
-            along = (onward >= 0) & (onward < lines)
-            if source is not None:
-                along = along & ((row - r) * step > 0)
-
-            @pl.when(along)
-            def _(way=way, onward=onward):
-                act(word_copy(source, r, way, at(onward, col, core)))
-
-        act(word_copy(source, r, 2, place + 1 - 2 * core))
 
     def weigh(k):
         load_copy(k).wait()
@@ -859,14 +862,10 @@
             def _(j):
                 weigh(s * (fold // PARTS) + j)
 
-        @pl.when(bearer & (n == lines) & (s == 0))
-        def _():
-            each_word(row, lambda c: c.start(), None)
-
         for sign in (1, -1):
             r = row + sign * s
 
-            @pl.when(bearer & (n == lines) & (s > 0) & (r >= 0) & (r < lines))
+            @pl.when(bearer & (n == 1) & (s > 0) & (r >= 0) & (r < lines))
             def _(r=r):
                 word_arrived(r)
                 each_word(r, lambda c: c.start())

time: 155 us -> 148 us (0.955)
  Pallas kernels: 150 us -> 144 us
    pallas_call x1, Pallas kernels: 66.2 us -> 58.5 us  [gather_scores(): pl.pallas_call(functools.partial(gather_kernel, orient), out_shape=(jax.S...]
where the time goes in v5:
time: 148 us
  Pallas kernels  144 us (97%)
  local copies, waits for them, and re-layouts  3.34 us (2%)
    pallas_call x1, Pallas kernels, gather_scores(): pl.pallas_call(functools.partial(gather_kernel, orient), out_shape=(jax.S...  58.5 us
    pallas_call x1, Pallas kernels, insert_data(): pl.pallas_call(data_kernel, grid=(steps,), out_shape=jax.ShapeDtypeStruct...  50.5 us
    pallas_call x1, Pallas kernels, reduce_rows(): pl.pallas_call(functools.partial(reduce_kernel, groups, orient), out_shap...  35 us
    unnamed x2, local copies, waits for them, and re-layouts  3.34 us

profile of v5, /device:TPU:0, one launch (start us, length us, event | category | flops | bytes accessed | tf_op | source)
XLA Modules:
  0.0 147.9 jit_solution(1008000057676664034)
XLA Ops:
  0.6 58.5 %shard_map.68 = (bf16[192,16384]{1,0:T(8,128)(2,1)}, bf16[256,192]{1,0:T(8,128)(2,1)}, f32[2,128]{1,0:T(2,128)}, s32[4,128,256]{2,1,0:T(8,128)}, s32[256,128]{1,0:T(8,128)}, /*index=5*/s32[8,128]{1,0:T(8,128)}) custom-call(bf16[12,16384]{1,0:T(8,128)(2,1)} %own_ref.1, bf16[256,16384]{1,0:T(8,128)(2,1)} %templates_ref.1, f32[1,16384]{1,0:T(1,128)} %bitcast.3, ...), custom_call_target="tpu_custom_call" | custom-call | tf_op jit(solution)/shard_map/pallas_call | solution.py:974
  59.1 50.5 %shard_map.69 = f32[16384,128]{1,0:T(8,128)} custom-call(bf16[256,192]{1,0:T(8,128)(2,1)} %get-tuple-element.8.post_ref, bf16[192,16384]{1,0:T(8,128)(2,1)} %get-tuple-element.9.images_ref, f32[256,128]{1,0:T(8,128)} %interp_ref.3, s32[256,128]{1,0:T(8,128)} %get-tuple-element.10.idx_ref, s32[8,128]{1,0:T(8,128)} %get-tuple-element.11.clash_ref), custom_call_target="tpu_custom_call" | custom-call | flops 199999995904 | bytes 200000000 | tf_op jit(solution)/shard_map/pallas_call | solution.py:104
  109.6 35.0 %shard_map.70 = (f32[512,128]{1,0:T(8,128)}, f32[512,128]{1,0:T(8,128)}) custom-call(f32[16,2,512,128]{3,2,1,0:T(8,128)} %bitcast.2, f32[2,128]{1,0:T(2,128)} %get-tuple-element.12.mass_ref, s32[4,128,256]{2,1,0:T(8,128)} %get-tuple-element.13.places_ref, f32[128,128]{1,0:T(8,128)} %noise_ref.1), custom_call_target="tpu_custom_call" | custom-call | tf_op jit(solution)/shard_map/pallas_call | solution.py:521
  144.5 1.7 %copy.9 = f32[512,128]{1,0:T(8,128)} copy(f32[512,128]{1,0:T(8,128)} %get-tuple-element.16) | data formatting | bytes 524288
  146.2 1.7 %copy.10 = f32[512,128]{1,0:T(8,128)} copy(f32[512,128]{1,0:T(8,128)} %get-tuple-element.17) | data formatting | bytes 524288

commit v6 on v5

--- a/solution.py
+++ b/solution.py
@@ -12,6 +12,9 @@
 ACCS = 4
 SUB = 4
 BATCH = 128
+SLOT = 512
+COLS = 2
+CHUNKS = 16
 LINES = 4
 PARTS = 4
 NORM_COLS = 1024
@@ -22,15 +25,36 @@
 VMEM_LIMIT = 56 * 2**20
 
 
-def data_kernel(post_ref, images_ref, interp_ref, idx_ref, clash_ref, out_ref, rows_ref, *more):
-    accs = (out_ref,) + more
-    step = pl.program_id(0)
+def data_kernel(
+    post_ref,
+    images_ref,
+    interp_ref,
+    idx_ref,
+    clash_ref,
+    out_ref,
+    rows_ref,
+    idx,
+    idx_sem,
+    out_sem,
+    *accs,
+):
+    step, steps = pl.program_id(0), pl.num_programs(0)
     count, side = post_ref.shape[0], out_ref.shape[1]
     volume_rows = out_ref.shape[0]
     halves = count // BATCH
+    slots = ROWS_STEP * count // SLOT
+    each = SLOT // BATCH
+
+    def fetch(at, u):
+        return pltpu.make_async_copy(
+            idx_ref.at[pl.ds((at * slots + u) * each, each)], idx.at[u], idx_sem.at[u]
+        )
 
     @pl.when(step == 0)
     def _():
+        for u in range(slots):
+            fetch(step, u).start()
+
         @pl.loop(0, volume_rows // 64)
         def _(c):
             rows = pl.ds(pl.multiple_of(c * 64, 64), 64)
@@ -38,85 +62,108 @@
                 acc[rows, :] = jnp.zeros((64, side), jnp.float32)
 
     interp = pltpu.roll(interp_ref[...], lax.rem(side - step * ROWS_STEP, side), axis=1)
-    for j in range(ROWS_STEP):
+    for j in range(0, ROWS_STEP, COLS):
         block = jnp.dot(
             post_ref[...],
-            images_ref[:, j * side : (j + 1) * side],
+            images_ref[:, j * side : (j + COLS) * side],
             preferred_element_type=jnp.float32,
         )
-        rows_ref[j * count : (j + 1) * count, :] = block * interp[:, j : j + 1]
-
-    @pl.loop(0, ROWS_STEP * halves)
-    def _(g):
-        base = pl.multiple_of(g * BATCH, BATCH)
-        voxels = idx_ref.at[g]
-        clash = clash_ref[lax.rem(g, halves), step * ROWS_STEP + lax.div(g, halves)]
-
-        @pl.when(clash == 0)
-        def _():
-            pending = [None] * ACCS
-
-            def flush(a):
-                for voxel, value in pending[a] or ():
-                    accs[a][pl.ds(voxel, 1), :] = value
-
-            for n in range(BATCH // SUB):
-                a = n % ACCS
-                flush(a)
-                pending[a] = []
-                for k in range(n * SUB, (n + 1) * SUB):
-                    voxel = voxels[k]
-                    value = accs[a][pl.ds(voxel, 1), :] + rows_ref[pl.ds(base + k, 1), :]
-                    pending[a].append((voxel, value))
-            for a in range(ACCS):
-                flush(a)
-
-        @pl.when(clash != 0)
-        def _():
-            @pl.loop(0, BATCH // ACCS)
-            def _(q):
-                first = q * ACCS
-                targets = [voxels[first + a] for a in range(ACCS)]
-                summed = [
-                    accs[a][pl.ds(targets[a], 1), :]
-                    + rows_ref[pl.ds(base + first + a, 1), :]
-                    for a in range(ACCS)
-                ]
+        for i in range(COLS):
+            rows_ref[(j + i) * count : (j + i + 1) * count, :] = (
+                block[:, i * side : (i + 1) * side] * interp[:, j + i : j + i + 1]
+            )
+
+    for u in range(slots):
+        fetch(step, u).wait()
+        for b in range(each):
+            base = (u * each + b) * BATCH
+            clash = clash_ref[b % halves, step * ROWS_STEP + base // count]
+
+            @pl.when(clash == 0)
+            def _(u=u, b=b, base=base):
+                pending = [()] * ACCS
+
+                def flush(a):
+                    for voxel, value in pending[a]:
+                        accs[a][pl.ds(voxel, 1), :] = value
+
+                for n in range(BATCH // SUB):
+                    a = n % ACCS
+                    flush(a)
+                    pending[a] = []
+                    for k in range(n * SUB, (n + 1) * SUB):
+                        voxel = idx[u, b, k]
+                        value = accs[a][pl.ds(voxel, 1), :] + rows_ref[base + k : base + k + 1, :]
+                        pending[a].append((voxel, value))
                 for a in range(ACCS):
-                    accs[a][pl.ds(targets[a], 1), :] = summed[a]
-
-    @pl.when(step == pl.num_programs(0) - 1)
+                    flush(a)
+
+            @pl.when(clash != 0)
+            def _(u=u, b=b, base=base):
+                @pl.loop(0, BATCH // ACCS)
+                def _(q):
+                    first = q * ACCS
+                    targets = [idx[u, b, first + a] for a in range(ACCS)]
+                    summed = [
+                        accs[a][pl.ds(targets[a], 1), :]
+                        + rows_ref[pl.ds(base + first + a, 1), :]
+                        for a in range(ACCS)
+                    ]
+                    for a in range(ACCS):
+                        accs[a][pl.ds(targets[a], 1), :] = summed[a]
+
+        @pl.when(step < steps - 1)
+        def _(u=u):
+            fetch(step + 1, u).start()
+
+    @pl.when(step == steps - 1)
     def _():
-        @pl.loop(0, volume_rows // 64)
-        def _(c):
-            rows = pl.ds(pl.multiple_of(c * 64, 64), 64)
-            total = accs[0][rows, :]
-            for acc in accs[1:]:
-                total = total + acc[rows, :]
-            out_ref[rows, :] = total
+        chunk = volume_rows // CHUNKS
+
+        def write(p):
+            rows = pl.ds(pl.multiple_of(p * chunk, chunk), chunk)
+            return pltpu.make_async_copy(accs[0].at[rows], out_ref.at[rows], out_sem.at[p])
+
+        @pl.loop(0, CHUNKS)
+        def _(p):
+            @pl.loop(0, chunk // 64)
+            def _(c):
+                rows = pl.ds(pl.multiple_of(p * chunk + c * 64, 64), 64)
+                total = accs[0][rows, :]
+                for acc in accs[1:]:
+                    total = total + acc[rows, :]
+                accs[0][rows, :] = total
+
+            write(p).start()
+
+        @pl.loop(0, CHUNKS)
+        def _(p):
+            write(p).wait()
 
 
 def insert_data(post, gathered, interp, voxels, clash, volume_rows):
     count, images = post.shape
     side = interp.shape[1]
-    steps = side // ROWS_STEP
-    batches = ROWS_STEP * count // BATCH
+    slots = ROWS_STEP * count // SLOT
     return pl.pallas_call(
         data_kernel,
-        grid=(steps,),
+        grid=(side // ROWS_STEP,),
         out_shape=jax.ShapeDtypeStruct((volume_rows, side), jnp.float32),
         in_specs=[
             pl.BlockSpec((count, images), lambda i: (0, 0)),
             pl.BlockSpec((images, ROWS_STEP * side), lambda i: (0, i)),
             pl.BlockSpec((count, side), lambda i: (0, 0)),
-            pl.BlockSpec((batches, BATCH), lambda i: (i, 0), memory_space=pltpu.SMEM),
+            pl.BlockSpec(memory_space=pl.ANY),
             pl.BlockSpec(memory_space=pltpu.SMEM),
         ],
-        out_specs=pl.BlockSpec(
-            (volume_rows, side), lambda i: (0, 0), pipeline_mode=pl.Buffered(1)
-        ),
-        scratch_shapes=[pltpu.VMEM((ROWS_STEP * count, side), jnp.float32)]
-        + [pltpu.VMEM((volume_rows, side), jnp.float32)] * (ACCS - 1),
+        out_specs=pl.BlockSpec(memory_space=pl.ANY),
+        scratch_shapes=[
+            pltpu.VMEM((ROWS_STEP * count, side), jnp.float32),
+            pltpu.SMEM((slots, SLOT // BATCH, BATCH), jnp.int32),
+            pltpu.SemaphoreType.DMA((slots,)),
+            pltpu.SemaphoreType.DMA((CHUNKS,)),
+        ]
+        + [pltpu.VMEM((volume_rows, side), jnp.float32)] * ACCS,
         compiler_params=pltpu.CompilerParams(vmem_limit_bytes=VMEM_LIMIT),
         cost_estimate=pl.CostEstimate(
             flops=200_000_000_000, bytes_accessed=200_000_000, transcendentals=0

time: 148 us -> 140 us (0.946)
  Pallas kernels: 144 us -> 136 us
    pallas_call x1, Pallas kernels: 50.5 us -> 41.6 us  [insert_data(): pl.pallas_call(data_kernel, grid=(side // ROWS_STEP,), out_shape=jax.Shap...]
where the time goes in v6:
time: 140 us
  Pallas kernels  136 us (97%)
  local copies, waits for them, and re-layouts  3.34 us (2%)
    pallas_call x1, Pallas kernels, gather_scores(): pl.pallas_call(functools.partial(gather_kernel, orient), out_shape=(jax.S...  58.5 us
    pallas_call x1, Pallas kernels, insert_data(): pl.pallas_call(data_kernel, grid=(side // ROWS_STEP,), out_shape=jax.Shap...  41.6 us
    pallas_call x1, Pallas kernels, reduce_rows(): pl.pallas_call(functools.partial(reduce_kernel, groups, orient), out_shap...  36.1 us
    unnamed x2, local copies, waits for them, and re-layouts  3.34 us

profile of v6, /device:TPU:0, one launch (start us, length us, event | category | flops | bytes accessed | tf_op | source)
XLA Modules:
  0.0 140.1 jit_solution(6063474434400742177)
XLA Ops:
  0.6 58.5 %shard_map.68 = (bf16[192,16384]{1,0:T(8,128)(2,1)}, bf16[256,192]{1,0:T(8,128)(2,1)}, f32[2,128]{1,0:T(2,128)}, s32[4,128,256]{2,1,0:T(8,128)}, s32[256,128]{1,0:T(8,128)}, /*index=5*/s32[8,128]{1,0:T(8,128)}) custom-call(bf16[12,16384]{1,0:T(8,128)(2,1)} %own_ref.1, bf16[256,16384]{1,0:T(8,128)(2,1)} %templates_ref.1, f32[1,16384]{1,0:T(1,128)} %bitcast.3, ...), custom_call_target="tpu_custom_call" | custom-call | tf_op jit(solution)/shard_map/pallas_call | solution.py:1021
  59.1 41.6 %shard_map.69 = f32[16384,128]{1,0:T(8,128)} custom-call(bf16[256,192]{1,0:T(8,128)(2,1)} %get-tuple-element.8.post_ref, bf16[192,16384]{1,0:T(8,128)(2,1)} %get-tuple-element.9.images_ref, f32[256,128]{1,0:T(8,128)} %interp_ref.3, s32[256,128]{1,0:T(8,128)} %get-tuple-element.10.idx_ref, s32[8,128]{1,0:T(8,128)} %get-tuple-element.11.clash_ref), custom_call_target="tpu_custom_call" | custom-call | flops 199999995904 | bytes 200000000 | tf_op jit(solution)/shard_map/pallas_call | solution.py:148
  100.7 36.1 %shard_map.70 = (f32[512,128]{1,0:T(8,128)}, f32[512,128]{1,0:T(8,128)}) custom-call(f32[16,2,512,128]{3,2,1,0:T(8,128)} %bitcast.2, f32[2,128]{1,0:T(2,128)} %get-tuple-element.12.mass_ref, s32[4,128,256]{2,1,0:T(8,128)} %get-tuple-element.13.places_ref, f32[128,128]{1,0:T(8,128)} %noise_ref.1), custom_call_target="tpu_custom_call" | custom-call | tf_op jit(solution)/shard_map/pallas_call | solution.py:568
  136.8 1.7 %copy.9 = f32[512,128]{1,0:T(8,128)} copy(f32[512,128]{1,0:T(8,128)} %get-tuple-element.16) | data formatting | bytes 524288
  138.5 1.7 %copy.10 = f32[512,128]{1,0:T(8,128)} copy(f32[512,128]{1,0:T(8,128)} %get-tuple-element.17) | data formatting | bytes 524288

commit v7 on v6

--- a/solution.py
+++ b/solution.py
@@ -15,6 +15,7 @@
 SLOT = 512
 COLS = 2
 CHUNKS = 16
+WORD_STEPS = 3
 LINES = 4
 PARTS = 4
 NORM_COLS = 1024
@@ -909,10 +910,11 @@
             def _(j):
                 weigh(s * (fold // PARTS) + j)
 
+        hop, early = lax.div(k, WORD_STEPS), lax.rem(k, WORD_STEPS)
         for sign in (1, -1):
-            r = row + sign * s
-
-            @pl.when(bearer & (n == 1) & (s > 0) & (r >= 0) & (r < lines))
+            r = row + sign * hop
+
+            @pl.when(bearer & (early == 0) & (hop > 0) & (hop < lines) & (r >= 0) & (r < lines))
             def _(r=r):
                 word_arrived(r)
                 each_word(r, lambda c: c.start())
@@ -1057,15 +1059,23 @@
     )(images, templates, noise_flat, index, interp)
 
 
+def finish_kernel(data_ref, weight_ref, data_out, weight_out):
+    data_out[...] = data_ref[...]
+    weight_out[...] = weight_ref[...]
+
+
+def finish(data, weight):
+    shape = jax.ShapeDtypeStruct(data.shape, data.dtype)
+    return pl.pallas_call(finish_kernel, out_shape=(shape, shape))(data, weight)
+
+
 def shards(groups, orient, images, templates, index, interp, inv_noise):
     side = inv_noise.shape[0]
     gathered, post, mass, places, voxels, clash = gather_scores(
         images, templates, index, interp, inv_noise.reshape(1, -1), orient
     )
     volume = insert_data(post, gathered, interp, voxels, clash, side * side)
-    return reduce_rows(
-        volume, mass, places, inv_noise, groups, orient
-    )
+    return finish(*reduce_rows(volume, mass, places, inv_noise, groups, orient))
 
 
 def solution(mesh):

time: 140 us -> 136 us (0.971)
  local copies, waits for them, and re-layouts: 3.34 us -> 0 us
    unnamed x2 -> x0, local copies, waits for them, and re-layouts: 3.34 us -> none
    pallas_call x1, Pallas kernels: 58.5 us -> 55.5 us  [gather_scores(): pl.pallas_call(functools.partial(gather_kernel, orient), out_shape=(jax.S...]
    pallas_call x0 -> x1, Pallas kernels: none -> 1.84 us  [finish(): return pl.pallas_call(finish_kernel, out_shape=(shape, shape))(data, weight)]
where the time goes in v7:
time: 136 us
  Pallas kernels  135 us (99%)
    pallas_call x1, Pallas kernels, gather_scores(): pl.pallas_call(functools.partial(gather_kernel, orient), out_shape=(jax.S...  55.5 us
    pallas_call x1, Pallas kernels, insert_data(): pl.pallas_call(data_kernel, grid=(side // ROWS_STEP,), out_shape=jax.Shap...  42.8 us
    pallas_call x1, Pallas kernels, reduce_rows(): pl.pallas_call(functools.partial(reduce_kernel, groups, orient), out_shap...  35.3 us

profile of v7, /device:TPU:0, one launch (start us, length us, event | category | flops | bytes accessed | tf_op | source)
XLA Modules:
  0.0 136.0 jit_solution(4923996652364165734)
XLA Ops:
  0.6 55.5 %shard_map.68 = (bf16[192,16384]{1,0:T(8,128)(2,1)}, bf16[256,192]{1,0:T(8,128)(2,1)}, f32[2,128]{1,0:T(2,128)}, s32[4,128,256]{2,1,0:T(8,128)}, s32[256,128]{1,0:T(8,128)}, /*index=5*/s32[8,128]{1,0:T(8,128)}) custom-call(bf16[12,16384]{1,0:T(8,128)(2,1)} %own_ref.1, bf16[256,16384]{1,0:T(8,128)(2,1)} %templates_ref.1, f32[1,16384]{1,0:T(1,128)} %bitcast.3, ...), custom_call_target="tpu_custom_call" | custom-call | tf_op jit(solution)/shard_map/pallas_call | solution.py:1023
  56.1 42.8 %shard_map.69 = f32[16384,128]{1,0:T(8,128)} custom-call(bf16[256,192]{1,0:T(8,128)(2,1)} %get-tuple-element.10.post_ref, bf16[192,16384]{1,0:T(8,128)(2,1)} %get-tuple-element.11.images_ref, f32[256,128]{1,0:T(8,128)} %interp_ref.3, s32[256,128]{1,0:T(8,128)} %get-tuple-element.12.idx_ref, s32[8,128]{1,0:T(8,128)} %get-tuple-element.13.clash_ref), custom_call_target="tpu_custom_call" | custom-call | flops 199999995904 | bytes 200000000 | tf_op jit(solution)/shard_map/pallas_call | solution.py:149
  98.9 35.3 %shard_map.70 = (f32[512,128]{1,0:T(8,128)}, f32[512,128]{1,0:T(8,128)}) custom-call(f32[16,2,512,128]{3,2,1,0:T(8,128)} %bitcast.2, f32[2,128]{1,0:T(2,128)} %get-tuple-element.14.mass_ref, s32[4,128,256]{2,1,0:T(8,128)} %get-tuple-element.15.places_ref, f32[128,128]{1,0:T(8,128)} %noise_ref.1), custom_call_target="tpu_custom_call" | custom-call | tf_op jit(solution)/shard_map/pallas_call | solution.py:569
  134.2 1.8 %shard_map.71 = (f32[512,128]{1,0:T(8,128)}, f32[512,128]{1,0:T(8,128)}) custom-call(f32[512,128]{1,0:T(8,128)} %get-tuple-element.16.data_ref, f32[512,128]{1,0:T(8,128)} %get-tuple-element.17.weight_ref), custom_call_target="tpu_custom_call" | custom-call | tf_op jit(solution)/shard_map/pallas_call | solution.py:1069

commit v8 on v7

--- a/solution.py
+++ b/solution.py
@@ -27,21 +27,27 @@
 
 
 def data_kernel(
-    post_ref,
-    images_ref,
-    interp_ref,
+    post_hbm,
+    images_hbm,
+    interp_hbm,
     idx_ref,
     clash_ref,
     out_ref,
     rows_ref,
+    post_ref,
+    images_two,
+    interp_ref,
     idx,
     idx_sem,
+    image_sem,
+    once_sem,
     out_sem,
     *accs,
 ):
     step, steps = pl.program_id(0), pl.num_programs(0)
     count, side = post_ref.shape[0], out_ref.shape[1]
     volume_rows = out_ref.shape[0]
+    wide = ROWS_STEP * side
     halves = count // BATCH
     slots = ROWS_STEP * count // SLOT
     each = SLOT // BATCH
@@ -51,8 +57,21 @@
             idx_ref.at[pl.ds((at * slots + u) * each, each)], idx.at[u], idx_sem.at[u]
         )
 
+    def load(at):
+        cols = pl.ds(pl.multiple_of(at * wide, wide), wide)
+        two = lax.rem(at, 2)
+        return pltpu.make_async_copy(
+            images_hbm.at[:, cols], images_two.at[two], image_sem.at[two]
+        )
+
+    post_copy = pltpu.make_async_copy(post_hbm, post_ref, once_sem.at[0])
+    interp_copy = pltpu.make_async_copy(interp_hbm, interp_ref, once_sem.at[1])
+
     @pl.when(step == 0)
     def _():
+        post_copy.start()
+        interp_copy.start()
+        load(step).start()
         for u in range(slots):
             fetch(step, u).start()
 
@@ -62,6 +81,16 @@
             for acc in accs:
                 acc[rows, :] = jnp.zeros((64, side), jnp.float32)
 
+        post_copy.wait()
+        interp_copy.wait()
+
+    load(step).wait()
+
+    @pl.when(step < steps - 1)
+    def _():
+        load(step + 1).start()
+
+    images_ref = images_two.at[lax.rem(step, 2)]
     interp = pltpu.roll(interp_ref[...], lax.rem(side - step * ROWS_STEP, side), axis=1)
     for j in range(0, ROWS_STEP, COLS):
         block = jnp.dot(
@@ -151,17 +180,22 @@
         grid=(side // ROWS_STEP,),
         out_shape=jax.ShapeDtypeStruct((volume_rows, side), jnp.float32),
         in_specs=[
-            pl.BlockSpec((count, images), lambda i: (0, 0)),
-            pl.BlockSpec((images, ROWS_STEP * side), lambda i: (0, i)),
-            pl.BlockSpec((count, side), lambda i: (0, 0)),
+            pl.BlockSpec(memory_space=pl.ANY),
+            pl.BlockSpec(memory_space=pl.ANY),
+            pl.BlockSpec(memory_space=pl.ANY),
             pl.BlockSpec(memory_space=pl.ANY),
             pl.BlockSpec(memory_space=pltpu.SMEM),
         ],
         out_specs=pl.BlockSpec(memory_space=pl.ANY),
         scratch_shapes=[
             pltpu.VMEM((ROWS_STEP * count, side), jnp.float32),
+            pltpu.VMEM((count, images), jnp.bfloat16),
+            pltpu.VMEM((2, images, ROWS_STEP * side), jnp.bfloat16),
+            pltpu.VMEM((count, side), jnp.float32),
             pltpu.SMEM((slots, SLOT // BATCH, BATCH), jnp.int32),
             pltpu.SemaphoreType.DMA((slots,)),
+            pltpu.SemaphoreType.DMA((2,)),
+            pltpu.SemaphoreType.DMA((2,)),
             pltpu.SemaphoreType.DMA((CHUNKS,)),
         ]
         + [pltpu.VMEM((volume_rows, side), jnp.float32)] * ACCS,
@@ -961,6 +995,35 @@
     def _():
         words_in[row] = words[...]
 
+    @pl.when(jnp.logical_not(bearer))
+    def _():
+        for r in range(lines):
+            word_arrived(r)
+
+    places_ref[...] = words_in[...]
+
+    @pl.when(bearer)
+    def _():
+        each_word(row, lambda c: c.wait_send(), None)
+        for r in range(lines):
+
+            @pl.when(row != r)
+            def _(r=r):
+                each_word(r, lambda c: c.wait_send())
+
+    for r in range(lines):
+        store_copy(r).wait()
+
+    @pl.loop(0, PARTS)
+    def _(s):
+        each_send(row, col, s, lambda c: c.wait_send(), None)
+        for r in range(lines):
+            for q in range(across):
+
+                @pl.when((row != r) | (col != q))
+                def _(r=r, q=q):
+                    each_send(r, q, s, lambda c: c.wait_send())
+
     @pl.loop(1, orient)
     def _(s):
         stat_copy(s).wait()
@@ -977,35 +1040,6 @@
     mass_t = jnp.broadcast_to(mass, (count, LANES)).T
     for h in range(count // LANES):
         mass_ref[h : h + 1, :] = mass_t[:1, h * LANES : (h + 1) * LANES]
-
-    @pl.when(jnp.logical_not(bearer))
-    def _():
-        for r in range(lines):
-            word_arrived(r)
-
-    places_ref[...] = words_in[...]
-
-    @pl.when(bearer)
-    def _():
-        each_word(row, lambda c: c.wait_send(), None)
-        for r in range(lines):
-
-            @pl.when(row != r)
-            def _(r=r):
-                each_word(r, lambda c: c.wait_send())
-
-    for r in range(lines):
-        store_copy(r).wait()
-
-    @pl.loop(0, PARTS)
-    def _(s):
-        each_send(row, col, s, lambda c: c.wait_send(), None)
-        for r in range(lines):
-            for q in range(across):
-
-                @pl.when((row != r) | (col != q))
-                def _(r=r, q=q):
-                    each_send(r, q, s, lambda c: c.wait_send())
 
 
 def gather_scores(images, templates, index, interp, noise_flat, orient):

time: 136 us -> 135 us (level)
    pallas_call x1, Pallas kernels: 35.3 us -> 37.4 us  [reduce_rows(): pl.pallas_call(functools.partial(reduce_kernel, groups, orient), out_shap...]
    pallas_call x1, Pallas kernels: 42.8 us -> 41 us  [insert_data(): pl.pallas_call(data_kernel, grid=(side // ROWS_STEP,), out_shape=jax.Shap...]
where the time goes in v8:
time: 135 us; the launch traced here: 136 us
  Pallas kernels  135 us (100%)
    pallas_call x1, Pallas kernels, gather_scores(): pl.pallas_call(functools.partial(gather_kernel, orient), out_shape=(jax.S...  54.7 us
    pallas_call x1, Pallas kernels, insert_data(): pl.pallas_call(data_kernel, grid=(side // ROWS_STEP,), out_shape=jax.Shap...  41 us
    pallas_call x1, Pallas kernels, reduce_rows(): pl.pallas_call(functools.partial(reduce_kernel, groups, orient), out_shap...  37.4 us

profile of v8, /device:TPU:0, one launch (start us, length us, event | category | flops | bytes accessed | tf_op | source)
XLA Modules:
  0.0 135.6 jit_solution(5627167207846833991)
XLA Ops:
  0.6 54.7 %shard_map.68 = (bf16[192,16384]{1,0:T(8,128)(2,1)}, bf16[256,192]{1,0:T(8,128)(2,1)}, f32[2,128]{1,0:T(2,128)}, s32[4,128,256]{2,1,0:T(8,128)}, s32[256,128]{1,0:T(8,128)}, /*index=5*/s32[8,128]{1,0:T(8,128)}) custom-call(bf16[12,16384]{1,0:T(8,128)(2,1)} %own_ref.1, bf16[256,16384]{1,0:T(8,128)(2,1)} %templates_ref.1, f32[1,16384]{1,0:T(1,128)} %bitcast.3, ...), custom_call_target="tpu_custom_call" | custom-call | tf_op jit(solution)/shard_map/pallas_call | solution.py:1057
  55.3 41.0 %shard_map.69 = f32[16384,128]{1,0:T(8,128)} custom-call(bf16[256,192]{1,0:T(8,128)(2,1)} %get-tuple-element.10.post_hbm, bf16[192,16384]{1,0:T(8,128)(2,1)} %get-tuple-element.11.images_hbm, f32[256,128]{1,0:T(8,128)} %interp_hbm.1, s32[256,128]{1,0:T(8,128)} %get-tuple-element.12.idx_ref, s32[8,128]{1,0:T(8,128)} %get-tuple-element.13.clash_ref), custom_call_target="tpu_custom_call" | custom-call | flops 199999995904 | bytes 200000000 | tf_op jit(solution)/shard_map/pallas_call | solution.py:178
  96.4 37.4 %shard_map.70 = (f32[512,128]{1,0:T(8,128)}, f32[512,128]{1,0:T(8,128)}) custom-call(f32[16,2,512,128]{3,2,1,0:T(8,128)} %bitcast.2, f32[2,128]{1,0:T(2,128)} %get-tuple-element.14.mass_ref, s32[4,128,256]{2,1,0:T(8,128)} %get-tuple-element.15.places_ref, f32[128,128]{1,0:T(8,128)} %noise_ref.1), custom_call_target="tpu_custom_call" | custom-call | tf_op jit(solution)/shard_map/pallas_call | solution.py:603
  133.8 1.8 %shard_map.71 = (f32[512,128]{1,0:T(8,128)}, f32[512,128]{1,0:T(8,128)}) custom-call(f32[512,128]{1,0:T(8,128)} %get-tuple-element.16.data_ref, f32[512,128]{1,0:T(8,128)} %get-tuple-element.17.weight_ref), custom_call_target="tpu_custom_call" | custom-call | tf_op jit(solution)/shard_map/pallas_call | solution.py:1103

commit v9 on v8

--- a/solution.py
+++ b/solution.py
@@ -211,10 +211,12 @@
     orient,
     blocks_ref,
     mass_ref,
-    places_ref,
+    places_hbm,
     noise_ref,
     out_ref,
     weight_ref,
+    places_ref,
+    places_sem,
     grid_ref,
     mass_row,
     mine,
@@ -308,6 +310,9 @@
             def _(k, i=i, j=j):
                 own_copy(k, i, j).start()
 
+    places_copy = pltpu.make_async_copy(places_hbm, places_ref, places_sem)
+    places_copy.start()
+
     pl.semaphore_wait(barrier, devices - 1)
 
     def mass_copy(s):
@@ -541,6 +546,8 @@
 
         @pl.when(slot == 1)
         def _():
+            places_copy.wait()
+
             @pl.when(core == lax.rem(group, 2))
             def _():
                 add_mass(rank, mass_ref)
@@ -606,13 +613,19 @@
             jax.ShapeDtypeStruct((rows, side), jnp.float32),
             jax.ShapeDtypeStruct((rows, side), jnp.float32),
         ),
-        in_specs=[pl.BlockSpec(memory_space=pl.ANY)]
-        + [pl.BlockSpec(memory_space=pltpu.VMEM)] * 3,
+        in_specs=[
+            pl.BlockSpec(memory_space=pl.ANY),
+            pl.BlockSpec(memory_space=pltpu.VMEM),
+            pl.BlockSpec(memory_space=pl.ANY),
+            pl.BlockSpec(memory_space=pltpu.VMEM),
+        ],
         out_specs=(
             pl.BlockSpec(memory_space=pltpu.VMEM),
             pl.BlockSpec(memory_space=pltpu.VMEM),
         ),
         scratch_shapes=[
+            pltpu.VMEM(places_t.shape, jnp.int32),
+            pltpu.SemaphoreType.DMA,
             pltpu.VMEM((2 * across * side * max(8, rows // LOW), LANES), jnp.float32),
             pltpu.VMEM((1, places_t.shape[0] * places_t.shape[2]), jnp.float32),
         ]

time: 135 us -> 135 us (level)
    pallas_call x1, Pallas kernels: 37.4 us -> 34.7 us  [reduce_rows(): pl.pallas_call(functools.partial(reduce_kernel, groups, orient), out_shap...]
    pallas_call x1, Pallas kernels: 41 us -> 42.8 us  [insert_data(): pl.pallas_call(data_kernel, grid=(side // ROWS_STEP,), out_shape=jax.Shap...]
where the time goes in v9:
time: 135 us
  Pallas kernels  134 us (99%)
    pallas_call x1, Pallas kernels, gather_scores(): pl.pallas_call(functools.partial(gather_kernel, orient), out_shape=(jax.S...  54.7 us
    pallas_call x1, Pallas kernels, insert_data(): pl.pallas_call(data_kernel, grid=(side // ROWS_STEP,), out_shape=jax.Shap...  42.8 us
    pallas_call x1, Pallas kernels, reduce_rows(): pl.pallas_call(functools.partial(reduce_kernel, groups, orient), out_shap...  34.7 us

profile of v9, /device:TPU:0, one launch (start us, length us, event | category | flops | bytes accessed | tf_op | source)
XLA Modules:
  0.0 134.6 jit_solution(1625079248969654751)
XLA Ops:
  0.6 54.7 %shard_map.68 = (bf16[192,16384]{1,0:T(8,128)(2,1)}, bf16[256,192]{1,0:T(8,128)(2,1)}, f32[2,128]{1,0:T(2,128)}, s32[4,128,256]{2,1,0:T(8,128)}, s32[256,128]{1,0:T(8,128)}, /*index=5*/s32[8,128]{1,0:T(8,128)}) custom-call(bf16[12,16384]{1,0:T(8,128)(2,1)} %own_ref.1, bf16[256,16384]{1,0:T(8,128)(2,1)} %templates_ref.1, f32[1,16384]{1,0:T(1,128)} %bitcast.3, ...), custom_call_target="tpu_custom_call" | custom-call | tf_op jit(solution)/shard_map/pallas_call | solution.py:1070
  55.3 42.8 %shard_map.69 = f32[16384,128]{1,0:T(8,128)} custom-call(bf16[256,192]{1,0:T(8,128)(2,1)} %get-tuple-element.10.post_hbm, bf16[192,16384]{1,0:T(8,128)(2,1)} %get-tuple-element.11.images_hbm, f32[256,128]{1,0:T(8,128)} %interp_hbm.1, s32[256,128]{1,0:T(8,128)} %get-tuple-element.12.idx_ref, s32[8,128]{1,0:T(8,128)} %get-tuple-element.13.clash_ref), custom_call_target="tpu_custom_call" | custom-call | flops 199999995904 | bytes 200000000 | tf_op jit(solution)/shard_map/pallas_call | solution.py:178
  98.1 34.7 %shard_map.70 = (f32[512,128]{1,0:T(8,128)}, f32[512,128]{1,0:T(8,128)}) custom-call(f32[16,2,512,128]{3,2,1,0:T(8,128)} %bitcast.2, f32[2,128]{1,0:T(2,128)} %get-tuple-element.14.mass_ref, s32[4,128,256]{2,1,0:T(8,128)} %get-tuple-element.15.places_hbm, f32[128,128]{1,0:T(8,128)} %noise_ref.1), custom_call_target="tpu_custom_call" | custom-call | tf_op jit(solution)/shard_map/pallas_call | solution.py:610
  132.8 1.8 %shard_map.71 = (f32[512,128]{1,0:T(8,128)}, f32[512,128]{1,0:T(8,128)}) custom-call(f32[512,128]{1,0:T(8,128)} %get-tuple-element.16.data_ref, f32[512,128]{1,0:T(8,128)} %get-tuple-element.17.weight_ref), custom_call_target="tpu_custom_call" | custom-call | tf_op jit(solution)/shard_map/pallas_call | solution.py:1116
